TPU v7x, 256 devices: a whole 4x4x8 slice. The times are simulated.
256 devices in a mesh: expert: 64 (over x, z, core), dp: 4 (over y).
Axes of the slice: x: 4, y: 4, z: 8, core: 2. Of those that a mesh axis runs over, the one named last changes fastest.
Arguments:
- tokens: bfloat16 [2048, 7168], P(('expert', 'dp')), may hold values from -6 to 6
- out_grads: bfloat16 [2048, 7168], P(('expert', 'dp')), may hold values from -4 to 4
- expert_ids: int32 [2048, 8], P('expert'), may hold values from 0 to 63, all different within a row; in each aligned block of 8 rows (0 to 7, 8 to 15, ...) at most 2 rows name the same one
- gates: bfloat16 [2048, 8], P('expert'), may hold values from 0.019897461 to 0.29882812
- w_gate: bfloat16 [64, 7168, 1024], P('expert', None, 'dp'), may hold values from -0.0625 to 0.0625
- w_up: bfloat16 [64, 7168, 1024], P('expert', None, 'dp'), may hold values from -0.0625 to 0.0625
- w_down: bfloat16 [64, 1024, 7168], P('expert', 'dp'), may hold values from -0.1875 to 0.1875
Outputs:
- input_grads: bfloat16 [2048, 7168], P(('expert', 'dp'))
- fisher: float32 [64], P('expert')
Inputs may be any that keep to these rules, and one draw needn't show every extreme that they name: `expert_ids`: each row names 8 different experts. In each aligned block of 8 rows no expert is named by more than 2 rows, a bound that some block reaches.
All inputs are finite; a program needn't handle non-finite values.
Results may differ from a plain program's by a relative error of at most 0.015.
Values may be sent and summed in bfloat16 or wider, within the bound.
A program may use at most 128 MiB of HBM per device.

v0:
```python
import jax
import jax.numpy as jnp
from jax import lax
from jax.sharding import PartitionSpec as P


def slot_numbers(route_ids, owners, capacity):
    experts_row = jnp.arange(owners, dtype=jnp.int32)
    hits = jnp.sum((route_ids[:, :, None] == experts_row).astype(jnp.int32), axis=1)
    earlier = jnp.cumsum(hits, axis=0) - hits
    ranks = jnp.take_along_axis(earlier, route_ids, axis=1)
    return route_ids * capacity + ranks


def slot_matches(route_ids, owners, capacity):
    slot_ids = slot_numbers(route_ids, owners, capacity)
    return slot_ids[None, :, :] == jnp.arange(owners * capacity, dtype=jnp.int32)[:, None, None]


def pack_rows(route_ids, gate_values, token_rows, grad_rows, owners, capacity):
    matches = slot_matches(route_ids, owners, capacity)
    picker = jnp.sum(matches.astype(jnp.float32), axis=2).astype(jnp.bfloat16)
    packed_tokens = jnp.dot(picker, token_rows, preferred_element_type=jnp.float32).astype(
        jnp.bfloat16
    )
    packed_grads = jnp.dot(picker, grad_rows, preferred_element_type=jnp.float32).astype(
        jnp.bfloat16
    )
    packed_gates = jnp.sum(
        jnp.where(matches, gate_values.astype(jnp.float32)[None], jnp.float32(0.0)), axis=(1, 2)
    ).astype(jnp.bfloat16)
    return (packed_tokens, packed_grads, packed_gates)


def times_transposed(left, right):
    return lax.dot_general(
        left, right, (((1,), (1,)), ((), ())), preferred_element_type=jnp.float32
    )


def per_device(tokens, out_grads, expert_ids, gates, w_gate, w_up, w_down):
    groups = lax.axis_size("dp")
    owners = lax.axis_size("expert")
    group_index = lax.axis_index("dp")
    rows_own = tokens.shape[0]
    feature_width = tokens.shape[1]
    choice_count = expert_ids.shape[1]
    capacity = min(rows_own, max(2, 2 * rows_own * choice_count // owners))
    slot_count = owners * capacity
    ids_groups = expert_ids.reshape(groups, rows_own, choice_count)
    gates_groups = gates.reshape(groups, rows_own, choice_count)
    ids_own = lax.dynamic_index_in_dim(ids_groups, group_index, 0, keepdims=False)
    gates_own = lax.dynamic_index_in_dim(gates_groups, group_index, 0, keepdims=False)
    all_tokens, all_grads = (
        lax.all_gather(tokens, "dp", axis=0, tiled=True),
        lax.all_gather(out_grads, "dp", axis=0, tiled=True),
    )

    def pack_group(route_ids, gate_values, token_rows, grad_rows):
        return pack_rows(route_ids, gate_values, token_rows, grad_rows, owners, capacity)

    packed_tokens, packed_grads, packed_gates = jax.vmap(pack_group)(
        ids_groups,
        gates_groups,
        all_tokens.reshape(groups, rows_own, feature_width),
        all_grads.reshape(groups, rows_own, feature_width),
    )
    routed_tokens, routed_grads, routed_gates = (
        lax.all_to_all(packed_tokens, "expert", split_axis=1, concat_axis=1, tiled=True),
        lax.all_to_all(packed_grads, "expert", split_axis=1, concat_axis=1, tiled=True),
        lax.all_to_all(packed_gates, "expert", split_axis=1, concat_axis=1, tiled=True),
    )
    total_rows = groups * slot_count
    token_rows = routed_tokens.reshape(total_rows, feature_width)
    grad_rows = routed_grads.reshape(total_rows, feature_width)
    row_gates = routed_gates.reshape(total_rows).astype(jnp.float32)
    gate_mat = w_gate[0]
    up_mat = w_up[0]
    down_mat = w_down[0]
    gate_pre = jnp.dot(token_rows, gate_mat, preferred_element_type=jnp.float32)
    up_pre = jnp.dot(token_rows, up_mat, preferred_element_type=jnp.float32)
    down_back = times_transposed(grad_rows, down_mat)
    sigmoid_a = jax.nn.sigmoid(gate_pre)
    active = gate_pre * sigmoid_a
    partial_dots = jnp.sum(active * up_pre * down_back, axis=1)
    d_gate = (down_back * up_pre * sigmoid_a * (1.0 + gate_pre * (1.0 - sigmoid_a))).astype(
        jnp.bfloat16
    )
    d_up = (down_back * active).astype(jnp.bfloat16)
    dots = lax.psum(partial_dots, "dp")
    fisher_local = jnp.sum((row_gates * dots) ** 2) * (1.0 / (rows_own * groups * choice_count))
    fisher = fisher_local.reshape(1)
    summed = times_transposed(d_gate, gate_mat) + times_transposed(d_up, up_mat)
    group_sums = lax.psum_scatter(
        lax.optimization_barrier(summed.astype(jnp.bfloat16))
        .astype(jnp.float32)
        .astype(jnp.bfloat16),
        "dp",
        scatter_dimension=0,
        tiled=True,
    )
    back_rows = lax.all_to_all(group_sums, "expert", split_axis=0, concat_axis=0, tiled=True)
    matches = slot_matches(ids_own, owners, capacity)
    combiner = jnp.sum(
        jnp.where(matches, gates_own.astype(jnp.float32)[None], jnp.float32(0.0)), axis=2
    )
    combined = lax.dot_general(
        combiner,
        back_rows.astype(jnp.float32),
        (((0,), (0,)), ((), ())),
        precision=lax.Precision.HIGHEST,
        preferred_element_type=jnp.float32,
    )
    return (combined.astype(jnp.bfloat16), fisher)


def solution(mesh):
    placed = (
        P(("expert", "dp"), None),
        P(("expert", "dp"), None),
        P("expert", None),
        P("expert", None),
        P("expert", None, "dp"),
        P("expert", None, "dp"),
        P("expert", "dp", None),
    )
    return jax.shard_map(
        per_device,
        mesh=mesh,
        in_specs=placed,
        out_specs=(P(("expert", "dp"), None), P("expert")),
        check_vma=False,
    )
```

profile of v0, /device:TPU:1, one launch (start us, length us, event | category | flops | bytes accessed | tf_op | source)
XLA Modules:
  0.0 560.3 jit_solution(13909217795693701320)
XLA Ops:
  7.2 0.8 copy.59
  7.9 0.8 copy.58
  8.7 0.1 convert_reduce_fusion.1
  8.9 0.1 reshape.159
  9.0 1.9 gather_fusion.1
  10.9 0.1 reshape.162
  11.0 12.3 %all_gather.7 = bf16[32,7168]{1,0:T(8,128)(2,1)S(1)} all-gather(bf16[8,7168]{1,0:T(8,128)(2,1)S(1)} %copy-done.4), channel_id=1, replica_groups=mesh['expert'=64,'dp'=4] {'dp'}, dimensions={0}, use_global_device_ids=true | all-gather | bytes 573440 | tf_op jit(solution)/shard_map/all_gather | solution.py:55
  23.3 0.1 select_reduce_fusion
  23.4 5.1 convolution_convert_fusion
  28.5 11.8 %copy.65 = bf16[4,128,7168]{2,0,1:T(4,128)(2,1)} copy(bf16[4,128,7168]{2,1,0:T(8,128)(2,1)} %convolution_convert_fusion) | data formatting | bytes 14680064 | tf_op jit(solution)/shard_map/vmap()/convert_element_type | solution.py:23
  40.3 14.1 %all-to-all-start.1 = ((bf16[4,128,7168]{2,0,1:T(4,128)(2,1)}), bf16[4,128,7168]{2,0,1:T(4,128)(2,1)}, u32[]{:S(2)}, u32[]{:S(2)}) async-start(bf16[4,128,7168]{2,0,1:T(4,128)(2,1)} %copy.65), calls=%async_computation.1 | async-start | bytes 14680064 | tf_op jit(solution)/shard_map/all_to_all | solution.py:69
  54.5 12.1 %all_gather.6 = bf16[32,7168]{1,0:T(8,128)(2,1)S(1)} all-gather(bf16[8,7168]{1,0:T(8,128)(2,1)S(1)} %copy-done.5), channel_id=1, replica_groups=mesh['expert'=64,'dp'=4] {'dp'}, dimensions={0}, use_global_device_ids=true | all-gather | bytes 573440 | tf_op jit(solution)/shard_map/all_gather | solution.py:56
  66.5 5.1 convolution_convert_fusion.1
  71.6 11.7 %copy.63 = bf16[4,128,7168]{2,0,1:T(4,128)(2,1)} copy(bf16[4,128,7168]{2,1,0:T(8,128)(2,1)} %convolution_convert_fusion.1) | data formatting | bytes 14680064 | tf_op jit(solution)/shard_map/vmap()/convert_element_type | solution.py:26
  83.3 134.5 %all-to-all-done.1 = bf16[4,128,7168]{2,0,1:T(4,128)(2,1)} async-done(((bf16[4,128,7168]{2,0,1:T(4,128)(2,1)}), bf16[4,128,7168]{2,0,1:T(4,128)(2,1)}, u32[]{:S(2)}, u32[]{:S(2)}) %all-to-all-start.1) | async-done | bytes 7340064 | tf_op jit(solution)/shard_map/all_to_all | solution.py:69
  217.8 6.0 %all-to-all-start = ((bf16[4,128,7168]{2,0,1:T(4,128)(2,1)}), bf16[4,128,7168]{2,0,1:T(4,128)(2,1)}, u32[]{:S(2)}, u32[]{:S(2)}) async-start(bf16[4,128,7168]{2,0,1:T(4,128)(2,1)} %copy.63), calls=%async_computation | async-start | bytes 14680064 | tf_op jit(solution)/shard_map/all_to_all | solution.py:70
  223.7 0.2 reduce-scatter.2.cloned.1.call-start
  224.0 0.0 copy-start.2
  224.0 5.4 copy.66
  229.4 0.0 copy-start
  229.4 2.1 fusion.2
  231.5 2.2 fusion.5
  233.7 153.4 %all-to-all-done = bf16[4,128,7168]{2,0,1:T(4,128)(2,1)} async-done(((bf16[4,128,7168]{2,0,1:T(4,128)(2,1)}), bf16[4,128,7168]{2,0,1:T(4,128)(2,1)}, u32[]{:S(2)}, u32[]{:S(2)}) %all-to-all-start) | async-done | bytes 7340064 | tf_op jit(solution)/shard_map/all_to_all | solution.py:70
  387.1 5.3 copy.64
  392.3 0.0 copy-start.3
  392.3 4.3 multiply_reduce_fusion
  396.7 0.0 copy-start.1
  396.7 7.8 %fusion = f32[512,7168]{1,0:T(8,128)} fusion(bf16[1,7168,256]{2,1,0:T(8,128)(2,1)S(1)} %copy-done.3, f32[512,256]{0,1:T(8,128)S(1)} %fusion.2, f32[512,256]{0,1:T(8,128)S(1)} %get-tuple-element.5, f32[512,256]{0,1:T(8,128)S(1)} %fusion.5), kind=kOutput, calls=%fused_computation.6 | convolution fusion | flops 1880358912 | bytes 19922944 | tf_op jit(solution)/shard_map/dot_general | solution.py:36
  404.4 10.5 %add_convert_fusion = bf16[512,7168]{1,0:T(8,128)(2,1)} fusion(f32[512,7168]{1,0:T(8,128)} %fusion, bf16[1,7168,256]{2,1,0:T(8,128)(2,1)S(1)} %copy-done.1, f32[512,256]{0,1:T(8,128)S(1)} %get-tuple-element.5, f32[512,256]{0,1:T(8,128)S(1)} %fusion.2), kind=kOutput, calls=%fused_computation.2 | convolution fusion | flops 1887174656 | bytes 26738688 | tf_op jit(solution)/shard_map/dot_general | solution.py:36
  414.9 0.0 reduce-scatter.2.cloned.1.call-update
  414.9 0.7 copy.67
  415.7 5.8 %all-to-all-start.3 = ((bf16[4,64,2]{0,2,1:T(2,128)(2,1)}), bf16[4,64,2]{0,2,1:T(2,128)(2,1)S(1)}, u32[]{:S(2)}, u32[]{:S(2)}) async-start(bf16[4,64,2]{0,2,1:T(2,128)(2,1)} %bitcast.13), calls=%async_computation.4 | async-start | bytes 65536 | tf_op jit(solution)/shard_map/all_to_all | solution.py:71
  421.5 65.3 %reduce-scatter.2.cloned.1.call-done = bf16[128,7168]{1,0:T(8,128)(2,1)} async-done(((bf16[512,7168]{1,0:T(8,128)(2,1)}), bf16[128,7168]{1,0:T(8,128)(2,1)}) %reduce-scatter.2.cloned.1.call-update) | async-done | bytes 1835024 | tf_op jit(solution)/shard_map/reduce_scatter | solution.py:94
  486.7 4.7 all_to_all.20
  491.5 10.6 %all-to-all-start.2 = ((bf16[64,2,7168]{2,1,0:T(2,128)(2,1)}), bf16[64,2,7168]{2,1,0:T(2,128)(2,1)S(1)}, u32[]{:S(2)}, u32[]{:S(2)}) async-start(bf16[64,2,7168]{2,1,0:T(2,128)(2,1)} %all_to_all.20), calls=%async_computation.3 | async-start | bytes 3670016 | tf_op jit(solution)/shard_map/all_to_all | solution.py:102
  502.1 0.1 convert_reduce_fusion.2
  502.2 0.1 reshape.153
  502.3 0.7 gather_fusion
  503.0 0.1 gather.11
  503.1 0.1 select_reduce_fusion.1
  503.2 0.1 copy.68
  503.3 0.1 copy.69
  503.5 0.1 reshape.152
  503.6 7.2 %psum.7 = f32[512]{0:T(512)S(1)} all-reduce(f32[512]{0:T(512)S(1)} %get-tuple-element.4), channel_id=1, replica_groups=mesh['expert'=64,'dp'=4] {'dp'}, use_global_device_ids=true, to_apply=%region_9.10 | all-reduce | flops 512 | bytes 4096 | tf_op jit(solution)/shard_map/psum | solution.py:90
  510.8 0.6 multiply_reduce_fusion.1
  512.0 35.4 %all-to-all-done.2 = bf16[64,2,7168]{2,1,0:T(2,128)(2,1)S(1)} async-done(((bf16[64,2,7168]{2,1,0:T(2,128)(2,1)}), bf16[64,2,7168]{2,1,0:T(2,128)(2,1)S(1)}, u32[]{:S(2)}, u32[]{:S(2)}) %all-to-all-start.2) | async-done | bytes 1835040 | tf_op jit(solution)/shard_map/all_to_all | solution.py:102
  547.5 1.7 all_to_all.22
  549.1 3.0 convolution_convert_fusion.2
  (20 shorter events, 0.2 us)
Async XLA Ops:
  9.0 2.0 copy-start.4
  40.3 14.2 %copy-start.5 = (bf16[8,7168]{1,0:T(8,128)(2,1)S(1)}, bf16[8,7168]{1,0:T(8,128)(2,1)}, u32[]{:S(2)}) copy-start(bf16[8,7168]{1,0:T(8,128)(2,1)} %param.8) | copy-start | bytes 344068
  40.3 177.5 %all-to-all-start.1 = ((bf16[4,128,7168]{2,0,1:T(4,128)(2,1)}), bf16[4,128,7168]{2,0,1:T(4,128)(2,1)}, u32[]{:S(2)}, u32[]{:S(2)}) async-start(bf16[4,128,7168]{2,0,1:T(4,128)(2,1)} %copy.65), calls=%async_computation.1 | async-start | bytes 14680064 | tf_op jit(solution)/shard_map/all_to_all | solution.py:69
  217.8 169.3 %all-to-all-start = ((bf16[4,128,7168]{2,0,1:T(4,128)(2,1)}), bf16[4,128,7168]{2,0,1:T(4,128)(2,1)}, u32[]{:S(2)}, u32[]{:S(2)}) async-start(bf16[4,128,7168]{2,0,1:T(4,128)(2,1)} %copy.63), calls=%async_computation | async-start | bytes 14680064 | tf_op jit(solution)/shard_map/all_to_all | solution.py:70
  223.7 263.0 %reduce-scatter.2.cloned.1.call-start = ((), (), s32[]{:S(2)}) async-start(), calls=%async_computation.5 | async-start | bytes 9175040 | tf_op jit(solution)/shard_map/reduce_scatter | solution.py:94
  224.0 5.4 copy-start.2
  229.4 2.1 copy-start
  392.3 4.3 copy-start.3
  396.7 7.8 %copy-start.1 = (bf16[1,7168,256]{2,1,0:T(8,128)(2,1)S(1)}, bf16[1,7168,256]{2,1,0:T(8,128)(2,1)}, u32[]{:S(2)}) copy-start(bf16[1,7168,256]{2,1,0:T(8,128)(2,1)} %param.12) | copy-start | bytes 11010052
  415.7 75.8 %all-to-all-start.3 = ((bf16[4,64,2]{0,2,1:T(2,128)(2,1)}), bf16[4,64,2]{0,2,1:T(2,128)(2,1)S(1)}, u32[]{:S(2)}, u32[]{:S(2)}) async-start(bf16[4,64,2]{0,2,1:T(2,128)(2,1)} %bitcast.13), calls=%async_computation.4 | async-start | bytes 65536 | tf_op jit(solution)/shard_map/all_to_all | solution.py:71
  491.5 56.0 %all-to-all-start.2 = ((bf16[64,2,7168]{2,1,0:T(2,128)(2,1)}), bf16[64,2,7168]{2,1,0:T(2,128)(2,1)S(1)}, u32[]{:S(2)}, u32[]{:S(2)}) async-start(bf16[64,2,7168]{2,1,0:T(2,128)(2,1)} %all_to_all.20), calls=%async_computation.3 | async-start | bytes 3670016 | tf_op jit(solution)/shard_map/all_to_all | solution.py:102
Sparse Core Ops, SparseCore 0:
  415.0 71.6 reduce-scatter.1
where the time goes:
time: 568 us; the launch traced here: 560 us
  waiting for transfers between devices  389 us (68%)
  local copies, waits for them, and re-layouts  46.1 us (8%)
  matrix products  39.9 us (7%)
  starting transfers between devices  36.7 us (6%)
  blocking collectives  31.6 us (6%)
  between operations  16.3 us (3%)
    all_to_all x1, waiting for transfers between devices, per_device(): lax.all_to_all(packed_grads, 'expert', split_axis=1, concat_axis=1, tiled...  153 us
    all_to_all x1, waiting for transfers between devices, per_device(): lax.all_to_all(packed_tokens, 'expert', split_axis=1, concat_axis=1, tile...  134 us
    reduce_scatter x1, waiting for transfers between devices, per_device(): lax.psum_scatter(lax.optimization_barrier(summed.astype(jnp.bfloat16)).as...  65.3 us
    all_to_all x1, waiting for transfers between devices, per_device(): lax.all_to_all(group_sums, 'expert', split_axis=0, concat_axis=0, tiled=T...  35.4 us
    dot_general x3, matrix products, times_transposed(): lax.dot_general(left, right, (((1,), (1,)), ((), ())), preferred_element_...  22.5 us
    all_to_all x1, starting transfers between devices, per_device(): lax.all_to_all(packed_tokens, 'expert', split_axis=1, concat_axis=1, tile...  14.1 us
    all_gather x1, blocking collectives, per_device(): lax.all_gather(tokens, 'dp', axis=0, tiled=True)  12.3 us
    all_gather x1, blocking collectives, per_device(): lax.all_gather(out_grads, 'dp', axis=0, tiled=True)  12.1 us
  transfers between devices with their start and end apart: 5, of which 4 were waited for; matrix products, arithmetic and copies ran while one was open for 5% of the time, Pallas kernels for 0%

commit v1 on v0

v1 whole, which is shorter than its diff:
```python
import functools

import jax
import jax.numpy as jnp
from jax import lax
from jax.experimental import pallas as pl
from jax.experimental.pallas import tpu as pltpu
from jax.sharding import PartitionSpec as P

F32, BF16 = jnp.float32, jnp.bfloat16
NX, NZ, NC, NY = 4, 8, 2, 4
META = 128
MESH = pl.DeviceIdType.MESH


def position():
    e = lax.axis_index("expert")
    return lax.div(e, NZ * NC), lax.rem(lax.div(e, NC), NZ), lax.rem(e, NC), lax.axis_index("dp")


def place(x, z, c, y):
    return {"expert": (x * NZ + z) * NC + c, "dp": y}


def remote(src, dst, send, recv, device):
    return pltpu.make_async_remote_copy(
        src_ref=src, dst_ref=dst, send_sem=send, recv_sem=recv, device_id=device, device_id_type=MESH
    )


def meet(peers):
    barrier = pltpu.get_barrier_semaphore()
    for peer in peers:
        pl.semaphore_signal(barrier, inc=1, device_id=peer, device_id_type=MESH)
    pl.semaphore_wait(barrier, len(peers))


def dot_nt(left, right):
    return lax.dot_general(left, right, (((1,), (1,)), ((), ())), preferred_element_type=F32)


def forward_kernel(
    chunks, blk, wg_hbm, wu_hbm, wd_hbm, da_ref, db_ref, sg_ref, un_ref,
    G, R, S, wg, wu, wd, acc, lsem, zs, zr, xs, xr, cs, cr, ys, yr,
):
    x, z, c, y = position()
    e = lax.axis_index("expert")
    nc = len(chunks)
    xp, xm, xa = lax.rem(x + 1, NX), lax.rem(x + NX - 1, NX), lax.rem(x + 2, NX)
    zp, zm = lax.rem(z + 1, NZ), lax.rem(z + NZ - 1, NZ)
    yp, ym, ya = lax.rem(y + 1, NY), lax.rem(y + NY - 1, NY), lax.rem(y + 2, NY)
    co = 1 - c
    dxp, dxm = place(xp, z, c, y), place(xm, z, c, y)
    dzp, dzm = place(x, zp, c, y), place(x, zm, c, y)
    dyp, dym = place(x, z, c, yp), place(x, z, c, ym)
    dco = place(x, z, co, y)
    loads = [
        pltpu.make_async_copy(wg_hbm, wg, lsem.at[0]),
        pltpu.make_async_copy(wu_hbm, wu, lsem.at[1]),
        pltpu.make_async_copy(wd_hbm, wd, lsem.at[2]),
    ]
    for load in loads:
        load.start()
    G[x, c, z] = blk[...]
    meet([dxp, dxm, dzp, dzm, dyp, dym, dco])
    sent = []

    def go(copy):
        copy.start()
        sent.append(copy)

    def cols(h):
        return pl.ds(chunks[h][0], chunks[h][1])

    def halves(h):
        start, size = chunks[h]
        first = size // 2 // 128 * 128
        return pl.ds(start, first), pl.ds(start + first, size - first)

    def zblock(h, off):
        return G.at[x, c, lax.rem(z + off + NZ, NZ), :, cols(h)]

    def z_send(h, step):
        if step < 4:
            b = zblock(h, -step)
            go(remote(b, b, zs.at[h, step], zr.at[h, step], dzp))
        if step < 3:
            b = zblock(h, step)
            go(remote(b, b, zs.at[h, 4 + step], zr.at[h, 4 + step], dzm))

    def z_recv(h, step):
        if step < 4:
            b = zblock(h, -step - 1)
            remote(b, b, zs.at[h, step], zr.at[h, step], dzp).wait_recv()
        if step < 3:
            b = zblock(h, step + 1)
            remote(b, b, zs.at[h, 4 + step], zr.at[h, 4 + step], dzm).wait_recv()

    def z_advance(h, step):
        z_recv(h, step)
        if step < 3:
            z_send(h, step + 1)

    def line(h, xx, cc):
        return G.at[xx, cc, :, :, cols(h)]

    def part(xx, ds):
        return G.at[xx, c, :, :, ds]

    def share(h, k, xx):
        b = line(h, xx, c)
        go(remote(b, b, cs.at[h, k], cr.at[h, k], dco))

    def shared(h, k, xx):
        b = line(h, xx, co)
        remote(b, b, cs.at[h, k], cr.at[h, k], dco).wait_recv()

    def x_start(h):
        b = line(h, x, c)
        go(remote(b, b, xs.at[h, 0], xr.at[h, 0], dxp))
        go(remote(b, b, xs.at[h, 1], xr.at[h, 1], dxm))
        share(h, 0, x)

    def x_forward(h):
        lo, hi = halves(h)
        b = line(h, xm, c)
        remote(b, b, xs.at[h, 0], xr.at[h, 0], dxp).wait_recv()
        go(remote(part(xm, lo), part(xm, lo), xs.at[h, 2], xr.at[h, 2], dxp))
        share(h, 1, xm)
        b = line(h, xp, c)
        remote(b, b, xs.at[h, 1], xr.at[h, 1], dxm).wait_recv()
        go(remote(part(xp, hi), part(xp, hi), xs.at[h, 3], xr.at[h, 3], dxm))
        share(h, 2, xp)

    def x_last(h):
        lo, hi = halves(h)
        remote(part(xa, lo), part(xa, lo), xs.at[h, 2], xr.at[h, 2], dxp).wait_recv()
        remote(part(xa, hi), part(xa, hi), xs.at[h, 3], xr.at[h, 3], dxm).wait_recv()
        share(h, 3, xa)

    rows = NC * NZ * 16

    def routes(xx):
        meta = G[xx, :, :, :, 0:META].reshape(rows, META).astype(F32)
        lane = lax.broadcasted_iota(jnp.int32, (rows, META), 1)
        chosen = jnp.where(lane < 8, meta, -1.0) == e.astype(F32)
        gates = pltpu.roll(meta, META - 8, 1)
        hit = jnp.sum(chosen.astype(F32), axis=1, keepdims=True)
        gate = jnp.sum(jnp.where(chosen, gates, 0.0), axis=1, keepdims=True)
        r = lax.broadcasted_iota(jnp.int32, (rows, rows), 0)
        q = lax.broadcasted_iota(jnp.int32, (rows, rows), 1)
        earlier = jnp.where((r // 8 == q // 8) & (q < r), 1.0, 0.0).astype(BF16)
        hits = jnp.broadcast_to(hit, (rows, META))
        rank = jnp.dot(earlier, hits.astype(BF16), preferred_element_type=F32)
        r = lax.broadcasted_iota(jnp.int32, (rows, META), 0)
        base = (r // 8 % 2) * 32 + (r // 128) * 16 + (r // 16 % 8) * 2
        match = (lane.astype(F32) == base.astype(F32) + rank) & (hits > 0.5)
        pick = jnp.where(match, 1.0, 0.0)
        S[xx] = jnp.transpose(pick)[:64].astype(BF16)
        give = jnp.where(match, jnp.broadcast_to(gate, (rows, META)), 0.0)
        un_ref[xx] = give.reshape(16, 16, META)[:, :8].reshape(128, META).astype(BF16)

    def pack(h, xx):
        if h == 0:
            routes(xx)
        slab = G[xx, :, :, :, cols(h)].reshape(rows, chunks[h][1])
        got = jnp.dot(S[xx], slab, preferred_element_type=F32).astype(BF16)
        R[y, xx, :, :, cols(h)] = got.reshape(2, 32, chunks[h][1])

    def packed(g, xx, ds):
        return R.at[g, xx, :, :, ds]

    def y_send(h, k, xx):
        b = packed(y, xx, cols(h))
        go(remote(b, b, ys.at[h, k, 0], yr.at[h, k, 0], dyp))
        go(remote(b, b, ys.at[h, k, 1], yr.at[h, k, 1], dym))

    def y_forward(h, k, xx):
        lo, hi = halves(h)
        b = packed(ym, xx, cols(h))
        remote(b, b, ys.at[h, k, 0], yr.at[h, k, 0], dyp).wait_recv()
        b = packed(ym, xx, lo)
        go(remote(b, b, ys.at[h, k, 2], yr.at[h, k, 2], dyp))
        b = packed(yp, xx, cols(h))
        remote(b, b, ys.at[h, k, 1], yr.at[h, k, 1], dym).wait_recv()
        b = packed(yp, xx, hi)
        go(remote(b, b, ys.at[h, k, 3], yr.at[h, k, 3], dym))

    def y_last(h, k, xx):
        lo, hi = halves(h)
        b = packed(ya, xx, lo)
        remote(b, b, ys.at[h, k, 2], yr.at[h, k, 2], dyp).wait_recv()
        b = packed(ya, xx, hi)
        remote(b, b, ys.at[h, k, 3], yr.at[h, k, 3], dym).wait_recv()

    order = [x, xm, xp, xa]

    def multiply(h):
        start, size = chunks[h]
        if h == 0:
            start, size = META, size - META
            for load in loads:
                load.wait()
        f = pl.ds(start - META, size)
        at = pl.ds(start, size)
        tok = R[:, :, 0, :, at].reshape(512, size)
        grad = R[:, :, 1, :, at].reshape(512, size)
        a = jnp.dot(tok, wg[f, :], preferred_element_type=F32)
        b = jnp.dot(tok, wu[f, :], preferred_element_type=F32)
        u = dot_nt(grad, wd[:, f])
        if h == 0:
            acc[0], acc[1], acc[2] = a, b, u
        else:
            acc[0] += a
            acc[1] += b
            acc[2] += u

    z_send(0, 0)
    for step in range(4):
        z_advance(0, step)
    x_start(0)
    waiting = []
    for h in range(nc):
        more = h + 1 < nc
        if more:
            z_send(h + 1, 0)
        shared(h, 0, x)
        pack(h, x)
        y_send(h, 0, x)
        if waiting:
            y_forward(*waiting.pop(0))
        if more:
            z_advance(h + 1, 0)
        x_forward(h)
        if more:
            z_advance(h + 1, 1)
        shared(h, 1, xm)
        pack(h, xm)
        y_send(h, 1, xm)
        y_forward(h, 0, x)
        if more:
            z_advance(h + 1, 2)
        shared(h, 2, xp)
        pack(h, xp)
        y_send(h, 2, xp)
        if more:
            z_advance(h + 1, 3)
            x_start(h + 1)
        x_last(h)
        y_forward(h, 1, xm)
        shared(h, 3, xa)
        pack(h, xa)
        y_send(h, 3, xa)
        y_forward(h, 2, xp)
        waiting.append((h, 3, xa))
        if h:
            for k, xx in enumerate(order):
                y_last(h - 1, k, xx)
            multiply(h - 1)
    y_forward(*waiting.pop(0))
    for k, xx in enumerate(order):
        y_last(nc - 1, k, xx)
    multiply(nc - 1)
    lane = lax.broadcasted_iota(jnp.int32, (128, META), 1)
    for g in range(4):
        at = pl.ds(g * 128, 128)
        a, b, u = acc[0, at, :], acc[1, at, :], acc[2, at, :]
        sig = jax.nn.sigmoid(a)
        active = a * sig
        s = jnp.sum(active * b * u, axis=1, keepdims=True)
        da_ref[at, :] = (u * b * sig * (1.0 + a * (1.0 - sig))).astype(BF16)
        db_ref[at, :] = (u * active).astype(BF16)
        meta = R[g, :, 0, :, 0:META].reshape(128, META).astype(F32)
        chosen = jnp.where(lane < 8, meta, -1.0) == e.astype(F32)
        gate = jnp.sum(jnp.where(chosen, pltpu.roll(meta, META - 8, 1), 0.0), axis=1, keepdims=True)
        sg_ref[at, :] = jnp.where(lane == 0, s, jnp.where(lane == 1, gate, 0.0))
    for copy in sent:
        copy.wait_send()


def forward(blk, wg, wu, wd, pieces):
    width = blk.shape[1] - META
    step = width // pieces
    chunks = [(META + i * step, step) for i in range(pieces)]
    chunks[0] = (0, META + step)
    vm = pl.BlockSpec(memory_space=pltpu.VMEM)
    hbm = pl.BlockSpec(memory_space=pl.ANY)
    D = pltpu.SemaphoreType.DMA
    shape = jax.ShapeDtypeStruct
    return pl.pallas_call(
        functools.partial(forward_kernel, chunks),
        out_shape=(
            shape((512, 256), BF16), shape((512, 256), BF16), shape((512, META), F32),
            shape((NX, 128, META), BF16),
        ),
        in_specs=[vm, hbm, hbm, hbm],
        out_specs=(vm, vm, vm, vm),
        scratch_shapes=[
            pltpu.VMEM((NX, NC, NZ, 16, width + META), BF16),
            pltpu.VMEM((NY, NX, 2, 32, width + META), BF16),
            pltpu.VMEM((NX, 64, 256), BF16),
            pltpu.VMEM((width, 256), BF16), pltpu.VMEM((width, 256), BF16), pltpu.VMEM((256, width), BF16),
            pltpu.VMEM((3, 512, 256), F32),
            D((3,)), D((pieces, 7)), D((pieces, 7)), D((pieces, 4)), D((pieces, 4)),
            D((pieces, 4)), D((pieces, 4)), D((pieces, 4, 4)), D((pieces, 4, 4)),
        ],
        compiler_params=pltpu.CompilerParams(
            collective_id=1, has_side_effects=True, vmem_limit_bytes=60 << 20
        ),
        name="forward",
    )(blk, wg, wu, wd)


def times_transposed(left, right):
    return lax.dot_general(left, right, (((1,), (1,)), ((), ())), preferred_element_type=F32)


def per_device(tokens, out_grads, expert_ids, gates, w_gate, w_up, w_down):
    group = lax.axis_index("dp")
    ids = lax.dynamic_slice_in_dim(expert_ids, group * 8, 8, 0).astype(BF16)
    own_gates = lax.dynamic_slice_in_dim(gates, group * 8, 8, 0)
    meta = jnp.pad(jnp.concatenate([ids, own_gates], axis=1), ((0, 0), (0, META - 16)))
    blk = jnp.concatenate(
        [jnp.concatenate([meta, meta], axis=0), jnp.concatenate([tokens, out_grads], axis=0)], axis=1
    )
    gate_mat, up_mat, down_mat = w_gate[0], w_up[0], w_down[0]
    d_gate, d_up, sg, give = forward(blk, gate_mat, up_mat, down_mat, 4)
    dots = lax.psum(sg[:, 0], "dp")
    fisher = (jnp.sum((sg[:, 1] * dots) ** 2) * (1.0 / 256.0)).reshape(1)
    summed = (times_transposed(d_gate, gate_mat) + times_transposed(d_up, up_mat)).astype(BF16)
    back = lax.psum_scatter(summed, "dp", scatter_dimension=0, tiled=True)
    back = back.reshape(NX, NC, NZ, 2, -1).transpose(0, 2, 1, 3, 4).reshape(64, 2, -1)
    rows = lax.all_to_all(back, "expert", split_axis=0, concat_axis=0, tiled=True)
    gv = give[:, :, :32].reshape(NX, NC, NZ, 8, NC, NZ, 2)
    gv = jnp.einsum("xczrczk->xzcrk", gv.astype(F32)).astype(BF16)
    gv = lax.all_to_all(gv.reshape(64, 8, 2), "expert", split_axis=0, concat_axis=0, tiled=True)
    out = jnp.einsum("erk,ekd->rd", gv, rows, preferred_element_type=F32)
    return (out.astype(BF16), fisher)


def solution(mesh):
    placed = (
        P(("expert", "dp"), None), P(("expert", "dp"), None), P("expert", None), P("expert", None),
        P("expert", None, "dp"), P("expert", None, "dp"), P("expert", "dp", None),
    )
    return jax.shard_map(
        per_device, mesh=mesh, in_specs=placed,
        out_specs=(P(("expert", "dp"), None), P("expert")), check_vma=False,
    )
```

time: 568 us -> 335 us (0.59); the launches traced: 560 us -> 334 us
  waiting for transfers between devices: 389 us -> 101 us
  Pallas kernels: 0 us -> 161 us
  local copies, waits for them, and re-layouts: 46.1 us -> 10.1 us
  blocking collectives: 31.6 us -> 7.19 us
  starting transfers between devices: 36.7 us -> 16.4 us
  matrix products: 39.9 us -> 20.1 us
    all_to_all x4 -> x2, waiting for transfers between devices: 323 us -> 36.7 us  [the longest x1 36.6 us: per_device(): lax.all_to_all(back, 'expert', split_axis=0, concat_axis=0, tiled=True)]
    pallas_call x0 -> x1, Pallas kernels: none -> 161 us  [forward(): pl.pallas_call(functools.partial(forward_kernel, chunks), out_shape=(shap...]
    all_gather x2 -> x0, blocking collectives: 24.4 us -> none  [the longest x1 12.3 us: per_device(): lax.all_gather(tokens, 'dp', axis=0, tiled=True)]
    convert_element_type x5 -> x3, local copies, waits for them, and re-layouts: 24.5 us -> 0.71 us  [per_device(): gv = jnp.einsum('xczrczk->xzcrk', gv.astype(F32)).astype(BF16)]
    all_to_all x4 -> x2, starting transfers between devices: 36.5 us -> 16.4 us  [the longest x1 10.6 us: per_device(): lax.all_to_all(back, 'expert', split_axis=0, concat_axis=0, tiled=True)]
    all_to_all x5 -> x0, local copies, waits for them, and re-layouts: 17.2 us -> none  [the longest x2 6.41 us: per_device(): lax.all_to_all(group_sums, 'expert', split_axis=0, concat_axis=0, tiled=T...]
    dot_general x5 -> x1, matrix products: 17.4 us -> 1.05 us  [per_device(): out = jnp.einsum('erk,ekd->rd', gv, rows, preferred_element_type=F32)]
    dot_general x3 -> x2, matrix products: 22.5 us -> 19.1 us  [times_transposed(): lax.dot_general(left, right, (((1,), (1,)), ((), ())), preferred_element_...]
  transfers between devices with their start and end apart: 5 -> 3, of which waited for: 4 -> 2; matrix products, arithmetic and copies ran while one was open for 5% -> 3% of each run, Pallas kernels for 0% -> 0%
where the time goes in v1:
time: 335 us; the launch traced here: 334 us
  Pallas kernels  161 us (48%)
  waiting for transfers between devices  101 us (30%)
  matrix products  20.1 us (6%)
  starting transfers between devices  16.4 us (5%)
  between operations  15.9 us (5%)
  local copies, waits for them, and re-layouts  10.1 us (3%)
  blocking collectives  7.19 us (2%)
    pallas_call x1, Pallas kernels, forward(): pl.pallas_call(functools.partial(forward_kernel, chunks), out_shape=(shap...  161 us
    reduce_scatter x1, waiting for transfers between devices, per_device(): back = lax.psum_scatter(summed, 'dp', scatter_dimension=0, tiled=True)  63.9 us
    all_to_all x1, waiting for transfers between devices, per_device(): lax.all_to_all(back, 'expert', split_axis=0, concat_axis=0, tiled=True)  36.6 us
    dot_general x2, matrix products, times_transposed(): lax.dot_general(left, right, (((1,), (1,)), ((), ())), preferred_element_...  19.1 us
    all_to_all x1, starting transfers between devices, per_device(): lax.all_to_all(back, 'expert', split_axis=0, concat_axis=0, tiled=True)  10.6 us
    psum x1, blocking collectives, per_device(): dots = lax.psum(sg[:, 0], 'dp')  7.19 us
  transfers between devices with their start and end apart: 3, of which 2 were waited for; matrix products, arithmetic and copies ran while one was open for 3% of the time, Pallas kernels for 0%

profile of v1, /device:TPU:1, one launch (start us, length us, event | category | flops | bytes accessed | tf_op | source)
XLA Modules:
  0.0 334.2 jit_solution(12623326643331034362)
XLA Ops:
  7.2 0.0 copy-start
  7.2 0.0 reduce-scatter.2.cloned.1.call-start
  7.2 0.8 constant_dynamic-slice_fusion
  8.0 0.1 copy.41
  8.1 0.0 copy-done
  8.1 0.1 constant_dynamic-slice_fusion.1
  8.1 0.1 copy.40
  8.2 0.1 fusion.5
  8.3 1.7 maximum_maximum_fusion.blk
  10.0 0.0 copy-start.2
  10.0 161.0 %forward.1 = (bf16[512,256]{1,0:T(8,128)(2,1)}, bf16[512,256]{1,0:T(8,128)(2,1)}, f32[512,128]{1,0:T(8,128)}, bf16[4,128,128]{2,1,0:T(8,128)(2,1)}) custom-call(bf16[16,7296]{1,0:T(8,128)(2,1)} %maximum_maximum_fusion.blk, bf16[7168,256]{1,0:T(8,128)(2,1)} %bitcast.23, bf16[7168,256]{1,0:T(8,128)(2,1)} %bitcast.22, bf16[256,7168]{1,0:T(8,128)(2,1)} %bitcast.25), custom_call_target="tpu_custom_call" | custom-call | tf_op jit(solution)/shard_map/forward/pallas_call | solution.py:290
  171.0 0.0 copy-done.2
  171.0 0.0 copy-start.1
  171.0 0.0 copy-start.4
  171.0 8.6 %fusion.7 = f32[512,7168]{1,0:T(8,128)} fusion(bf16[512,256]{1,0:T(8,128)(2,1)} %get-tuple-element.7, bf16[1,7168,256]{2,1,0:T(8,128)(2,1)S(1)} %copy-done.2), kind=kOutput, calls=%fused_computation.22 | convolution fusion | flops 1879048192 | bytes 18612224 | tf_op jit(solution)/shard_map/dot_general | solution.py:315
  179.6 0.0 copy-done.1
  179.6 0.0 copy-done.4
  179.6 10.5 %add_convert_fusion = bf16[512,7168]{1,0:T(8,128)(2,1)} fusion(f32[512,7168]{1,0:T(8,128)} %fusion.7, bf16[512,256]{1,0:T(8,128)(2,1)S(1)} %copy-done.4, bf16[1,7168,256]{2,1,0:T(8,128)(2,1)S(1)} %copy-done.1), kind=kOutput, calls=%fused_computation | convolution fusion | flops 1886388224 | bytes 25952256 | tf_op jit(solution)/shard_map/dot_general | solution.py:315
  190.1 0.0 copy-start.5
  190.1 0.0 reduce-scatter.2.cloned.1.call-update
  190.1 0.9 copy-done.5
  191.0 0.1 copy.34
  191.1 0.6 reshape.23
  191.8 0.2 select_reduce_fusion
  192.0 0.3 select_reduce_fusion.1
  192.3 0.6 copy.36
  192.9 5.8 %all-to-all-start = ((bf16[64,8,2]{1,2,0:T(2,128)(2,1)}), bf16[64,8,2]{1,2,0:T(2,128)(2,1)S(1)}, u32[]{:S(2)}, u32[]{:S(2)}) async-start(bf16[64,8,2]{1,2,0:T(2,128)(2,1)} %copy.36), calls=%async_computation | async-start | bytes 65536 | tf_op jit(solution)/shard_map/all_to_all | solution.py:336
  198.7 63.9 %reduce-scatter.2.cloned.1.call-done = bf16[128,7168]{1,0:T(8,128)(2,1)} async-done(((bf16[512,7168]{1,0:T(8,128)(2,1)}), bf16[128,7168]{1,0:T(8,128)(2,1)}) %reduce-scatter.2.cloned.1.call-update) | async-done | bytes 1835024 | tf_op jit(solution)/shard_map/reduce_scatter | solution.py:331
  262.6 3.9 %reshape.20 = bf16[4,2,8,2,7168]{4,3,2,1,0:T(2,128)(2,1)S(1)} reshape(bf16[128,7168]{1,0:T(8,128)(2,1)} %reduce-scatter.2.cloned.1.call-done) | data formatting | bytes 3670016 | tf_op jit(solution)/shard_map/reshape | solution.py:332
  266.5 0.0 copy-start.3
  266.5 2.7 copy.37
  269.2 0.0 all-to-all-done
  269.2 10.6 %all-to-all-start.1 = ((bf16[64,2,7168]{2,1,0:T(2,128)(2,1)}), bf16[64,2,7168]{2,1,0:T(2,128)(2,1)S(1)}, u32[]{:S(2)}, u32[]{:S(2)}) async-start(bf16[64,2,7168]{2,1,0:T(2,128)(2,1)} %bitcast.6), calls=%async_computation.2 | async-start | bytes 3670016 | tf_op jit(solution)/shard_map/all_to_all | solution.py:333
  279.8 0.0 copy-done.3
  279.8 0.3 slice_reduce_fusion
  280.1 7.2 %psum.7 = f32[512]{0:T(512)S(1)} all-reduce(f32[512]{0:T(512)S(1)} %get-tuple-element.10), channel_id=1, replica_groups=mesh['expert'=64,'dp'=4] {'dp'}, use_global_device_ids=true, to_apply=%region_3.4 | all-reduce | flops 512 | bytes 4096 | tf_op jit(solution)/shard_map/psum | solution.py:328
  287.3 0.6 multiply_reduce_fusion
  288.5 36.6 %all-to-all-done.1 = bf16[64,2,7168]{2,1,0:T(2,128)(2,1)S(1)} async-done(((bf16[64,2,7168]{2,1,0:T(2,128)(2,1)}), bf16[64,2,7168]{2,1,0:T(2,128)(2,1)S(1)}, u32[]{:S(2)}, u32[]{:S(2)}) %all-to-all-start.1) | async-done | bytes 1835040 | tf_op jit(solution)/shard_map/all_to_all | solution.py:333
  325.2 1.0 fusion
  (5 shorter events, 0.1 us)
Async XLA Ops:
  7.2 0.9 copy-start
  7.2 255.4 %reduce-scatter.2.cloned.1.call-start = ((), (), s32[]{:S(2)}) async-start(), calls=%async_computation.3 | async-start | bytes 9175040 | tf_op jit(solution)/shard_map/reduce_scatter | solution.py:331
  10.0 161.0 %copy-start.2 = (bf16[1,7168,256]{2,1,0:T(8,128)(2,1)S(1)}, bf16[1,7168,256]{2,1,0:T(8,128)(2,1)}, u32[]{:S(2)}) copy-start(bf16[1,7168,256]{2,1,0:T(8,128)(2,1)} %param.11) | copy-start | bytes 11010052
  171.0 8.7 %copy-start.1 = (bf16[1,7168,256]{2,1,0:T(8,128)(2,1)S(1)}, bf16[1,7168,256]{2,1,0:T(8,128)(2,1)}, u32[]{:S(2)}) copy-start(bf16[1,7168,256]{2,1,0:T(8,128)(2,1)} %param.12) | copy-start | bytes 11010052
  171.0 8.6 %copy-start.4 = (bf16[512,256]{1,0:T(8,128)(2,1)S(1)}, bf16[512,256]{1,0:T(8,128)(2,1)}, u32[]{:S(2)}) copy-start(bf16[512,256]{1,0:T(8,128)(2,1)} %get-tuple-element.8) | copy-start | bytes 786436
  190.1 0.9 copy-start.5
  192.9 76.3 %all-to-all-start = ((bf16[64,8,2]{1,2,0:T(2,128)(2,1)}), bf16[64,8,2]{1,2,0:T(2,128)(2,1)S(1)}, u32[]{:S(2)}, u32[]{:S(2)}) async-start(bf16[64,8,2]{1,2,0:T(2,128)(2,1)} %copy.36), calls=%async_computation | async-start | bytes 65536 | tf_op jit(solution)/shard_map/all_to_all | solution.py:336
  266.5 13.3 %copy-start.3 = (f32[512,128]{1,0:T(8,128)S(1)}, f32[512,128]{1,0:T(8,128)}, u32[]{:S(2)}) copy-start(f32[512,128]{1,0:T(8,128)} %get-tuple-element.9) | copy-start | bytes 786436
  269.2 56.0 %all-to-all-start.1 = ((bf16[64,2,7168]{2,1,0:T(2,128)(2,1)}), bf16[64,2,7168]{2,1,0:T(2,128)(2,1)S(1)}, u32[]{:S(2)}, u32[]{:S(2)}) async-start(bf16[64,2,7168]{2,1,0:T(2,128)(2,1)} %bitcast.6), calls=%async_computation.2 | async-start | bytes 3670016 | tf_op jit(solution)/shard_map/all_to_all | solution.py:333
Sparse Core Ops, SparseCore 0:
  190.3 72.3 reduce-scatter.1

commit v2 on v1

--- a/solution.py
+++ b/solution.py
@@ -10,6 +10,7 @@
 F32, BF16 = jnp.float32, jnp.bfloat16
 NX, NZ, NC, NY = 4, 8, 2, 4
 META = 128
+FORWARD_PIECES, BACKWARD_PIECES = 4, 7
 MESH = pl.DeviceIdType.MESH
 
 
@@ -273,7 +274,7 @@
         meta = R[g, :, 0, :, 0:META].reshape(128, META).astype(F32)
         chosen = jnp.where(lane < 8, meta, -1.0) == e.astype(F32)
         gate = jnp.sum(jnp.where(chosen, pltpu.roll(meta, META - 8, 1), 0.0), axis=1, keepdims=True)
-        sg_ref[at, :] = jnp.where(lane == 0, s, jnp.where(lane == 1, gate, 0.0))
+        sg_ref[g] = jnp.transpose(jnp.where(lane == 0, s, jnp.where(lane == 1, gate, 0.0)))[:8]
     for copy in sent:
         copy.wait_send()
 
@@ -290,7 +291,7 @@
     return pl.pallas_call(
         functools.partial(forward_kernel, chunks),
         out_shape=(
-            shape((512, 256), BF16), shape((512, 256), BF16), shape((512, META), F32),
+            shape((512, 256), BF16), shape((512, 256), BF16), shape((NY, 8, META), F32),
             shape((NX, 128, META), BF16),
         ),
         in_specs=[vm, hbm, hbm, hbm],
@@ -311,8 +312,185 @@
     )(blk, wg, wu, wd)
 
 
-def times_transposed(left, right):
-    return lax.dot_general(left, right, (((1,), (1,)), ((), ())), preferred_element_type=F32)
+def backward_kernel(
+    chunks, da, db, sg, un, wg_hbm, wu_hbm, out_ref, fis_ref,
+    O, R1, R2, E, DS, RC, X1, X2, Fz, RZ, SB, wg, wu,
+    lsem, ss, sr, ys, yr, cs, cr, xs, xr, zs, zr,
+):
+    x, z, c, y = position()
+    nc = len(chunks)
+    xp, xm, xa = lax.rem(x + 1, NX), lax.rem(x + NX - 1, NX), lax.rem(x + 2, NX)
+    zp, zm = lax.rem(z + 1, NZ), lax.rem(z + NZ - 1, NZ)
+    yp, ym, ya = lax.rem(y + 1, NY), lax.rem(y + NY - 1, NY), lax.rem(y + 2, NY)
+    co = 1 - c
+    dxp, dxm = place(xp, z, c, y), place(xm, z, c, y)
+    dzp, dzm = place(x, zp, c, y), place(x, zm, c, y)
+    dyp, dym, dya = place(x, z, c, yp), place(x, z, c, ym), place(x, z, c, ya)
+    dco = place(x, z, co, y)
+
+    def rows_of(h):
+        return pl.ds(chunks[h][0], chunks[h][1])
+
+    loads = []
+    for h in range(nc):
+        for i, (src, dst) in enumerate(((wg_hbm, wg), (wu_hbm, wu))):
+            load = pltpu.make_async_copy(src.at[rows_of(h), :], dst.at[rows_of(h), :], lsem.at[h, i])
+            load.start()
+            loads.append(load)
+    SB[y] = sg[...]
+    meet([dxp, dxm, dzp, dzm, dyp, dym, dya, dco])
+    sent = []
+
+    def go(copy):
+        copy.start()
+        sent.append(copy)
+
+    def got(dst, send, recv, device):
+        remote(dst, dst, send, recv, device).wait_recv()
+
+    score = [(dyp, ym), (dym, yp), (dya, ya)]
+    for i, (device, _) in enumerate(score):
+        go(remote(SB.at[y], SB.at[y], ss.at[i], sr.at[i], device))
+
+    def halves(h):
+        start, size = chunks[h]
+        return pl.ds(start, size // 2), pl.ds(start + size // 2, size // 2)
+
+    def half(h):
+        start, size = chunks[h]
+        return pl.ds(start // 2, size // 2)
+
+    def up(v):
+        return v.astype(F32)
+
+    def stage_a(h):
+        at = rows_of(h)
+        loads[2 * h].wait()
+        loads[2 * h + 1].wait()
+        part = dot_nt(da[...], wg[at, :]) + dot_nt(db[...], wu[at, :])
+        O[:, :, :, at] = part.astype(BF16).reshape(NY, NX, 32, chunks[h][1])
+        lo, hi = halves(h)
+        go(remote(O.at[ya, :, :, lo], R1.at[0, :, :, half(h)], ys.at[h, 0], yr.at[h, 0], dyp))
+        go(remote(O.at[ya, :, :, hi], R1.at[1, :, :, half(h)], ys.at[h, 1], yr.at[h, 1], dym))
+
+    def stage_b(h):
+        at = rows_of(h)
+        lo, hi = halves(h)
+        got(R1.at[0, :, :, half(h)], ys.at[h, 0], yr.at[h, 0], dyp)
+        O[yp, :, :, lo] = (up(O[yp, :, :, lo]) + up(R1[0, :, :, half(h)])).astype(BF16)
+        go(remote(O.at[yp, :, :, at], R2.at[0, :, :, at], ys.at[h, 2], yr.at[h, 2], dyp))
+        got(R1.at[1, :, :, half(h)], ys.at[h, 1], yr.at[h, 1], dym)
+        O[ym, :, :, hi] = (up(O[ym, :, :, hi]) + up(R1[1, :, :, half(h)])).astype(BF16)
+        go(remote(O.at[ym, :, :, at], R2.at[1, :, :, at], ys.at[h, 3], yr.at[h, 3], dym))
+
+    def stage_c(h):
+        at = rows_of(h)
+        got(R2.at[0, :, :, at], ys.at[h, 2], yr.at[h, 2], dyp)
+        got(R2.at[1, :, :, at], ys.at[h, 3], yr.at[h, 3], dym)
+        for t in range(NX):
+            back = (up(O[y, t, :, at]) + up(R2[0, t, :, at]) + up(R2[1, t, :, at])).astype(BF16)
+            mine = un[t, pl.ds(pl.multiple_of(c * 64, 64), 64), :][:, :32]
+            theirs = un[t, pl.ds(pl.multiple_of(co * 64, 64), 64), :][:, :32]
+            DS[t, :, at] = jnp.dot(theirs, back, preferred_element_type=F32).astype(BF16)
+            E[t, :, at] = jnp.dot(mine, back, preferred_element_type=F32).astype(BF16)
+        go(remote(DS.at[:, :, at], RC.at[:, :, at], cs.at[h], cr.at[h], dco))
+
+    def stage_d(h):
+        at = rows_of(h)
+        lo, hi = halves(h)
+        got(RC.at[:, :, at], cs.at[h], cr.at[h], dco)
+        E[:, :, at] = (up(E[:, :, at]) + up(RC[:, :, at])).astype(BF16)
+        go(remote(E.at[xa, :, lo], X1.at[0, :, half(h)], xs.at[h, 0], xr.at[h, 0], dxp))
+        go(remote(E.at[xa, :, hi], X1.at[1, :, half(h)], xs.at[h, 1], xr.at[h, 1], dxm))
+
+    def stage_e(h):
+        at = rows_of(h)
+        lo, hi = halves(h)
+        got(X1.at[0, :, half(h)], xs.at[h, 0], xr.at[h, 0], dxp)
+        E[xp, :, lo] = (up(E[xp, :, lo]) + up(X1[0, :, half(h)])).astype(BF16)
+        go(remote(E.at[xp, :, at], X2.at[0, :, at], xs.at[h, 2], xr.at[h, 2], dxp))
+        got(X1.at[1, :, half(h)], xs.at[h, 1], xr.at[h, 1], dxm)
+        E[xm, :, hi] = (up(E[xm, :, hi]) + up(X1[1, :, half(h)])).astype(BF16)
+        go(remote(E.at[xm, :, at], X2.at[1, :, at], xs.at[h, 3], xr.at[h, 3], dxm))
+
+    def zrow(off):
+        return lax.rem(z + off + NZ, NZ)
+
+    def z_send(h, step):
+        at = rows_of(h)
+        if step < 4:
+            go(remote(Fz.at[zrow(4 - step), :, at], RZ.at[step, :, at], zs.at[h, step], zr.at[h, step], dzp))
+        if step < 3:
+            go(remote(Fz.at[zrow(step - 3), :, at], RZ.at[4 + step, :, at], zs.at[h, 4 + step], zr.at[h, 4 + step], dzm))
+
+    def stage_f(h):
+        at = rows_of(h)
+        got(X2.at[0, :, at], xs.at[h, 2], xr.at[h, 2], dxp)
+        got(X2.at[1, :, at], xs.at[h, 3], xr.at[h, 3], dxm)
+        total = up(E[x, :, at]) + up(X2[0, :, at]) + up(X2[1, :, at])
+        Fz[:, :, at] = total.reshape(NZ, 8, chunks[h][1])
+        z_send(h, 0)
+
+    def stage_z(step):
+        def run(h):
+            at = rows_of(h)
+            got(RZ.at[step - 1, :, at], zs.at[h, step - 1], zr.at[h, step - 1], dzp)
+            Fz[zrow(4 - step), :, at] += RZ[step - 1, :, at]
+            if step < 4:
+                got(RZ.at[3 + step, :, at], zs.at[h, 3 + step], zr.at[h, 3 + step], dzm)
+                Fz[zrow(step - 3), :, at] += RZ[3 + step, :, at]
+                if step < 3:
+                    z_send(h, step)
+                else:
+                    go(remote(Fz.at[zrow(1), :, at], RZ.at[3, :, at], zs.at[h, 3], zr.at[h, 3], dzp))
+            else:
+                out_ref[:, at] = Fz[z, :, at].astype(BF16)
+        return run
+
+    stages = [stage_a, stage_b, stage_c, stage_d, stage_e, stage_f] + [stage_z(i) for i in (1, 2, 3, 4)]
+    for i in range(nc + len(stages) - 1):
+        for lag, stage in enumerate(stages):
+            if 0 <= i - lag < nc:
+                stage(i - lag)
+    for i, (device, who) in enumerate(score):
+        got(SB.at[who], ss.at[i], sr.at[i], device)
+    dots = SB[0, :, 0, :] + SB[1, :, 0, :] + SB[2, :, 0, :] + SB[3, :, 0, :]
+    fis_ref[0] = jnp.sum((sg[:, 1, :] * dots) ** 2) * (1.0 / 256.0)
+    for copy in sent:
+        copy.wait_send()
+
+
+def backward(da, db, sg, un, wg, wu, pieces):
+    width = wg.shape[0]
+    step = width // pieces
+    chunks = [(i * step, step) for i in range(pieces)]
+    vm = pl.BlockSpec(memory_space=pltpu.VMEM)
+    hbm = pl.BlockSpec(memory_space=pl.ANY)
+    D = pltpu.SemaphoreType.DMA
+    return pl.pallas_call(
+        functools.partial(backward_kernel, chunks),
+        out_shape=(jax.ShapeDtypeStruct((8, width), BF16), jax.ShapeDtypeStruct((1,), F32)),
+        in_specs=[vm, vm, vm, vm, hbm, hbm],
+        out_specs=(vm, pl.BlockSpec(memory_space=pltpu.SMEM)),
+        scratch_shapes=[
+            pltpu.VMEM((NY, NX, 32, width), BF16),
+            pltpu.VMEM((2, NX, 32, width // 2), BF16),
+            pltpu.VMEM((2, NX, 32, width), BF16),
+            pltpu.VMEM((NX, 64, width), BF16), pltpu.VMEM((NX, 64, width), BF16), pltpu.VMEM((NX, 64, width), BF16),
+            pltpu.VMEM((2, 64, width // 2), BF16),
+            pltpu.VMEM((2, 64, width), BF16),
+            pltpu.VMEM((NZ, 8, width), F32),
+            pltpu.VMEM((7, 8, width), F32),
+            pltpu.VMEM((NY, NY, 8, META), F32),
+            pltpu.VMEM((width, 256), BF16), pltpu.VMEM((width, 256), BF16),
+            D((pieces, 2)), D((3,)), D((3,)), D((pieces, 4)), D((pieces, 4)), D((pieces,)), D((pieces,)),
+            D((pieces, 4)), D((pieces, 4)), D((pieces, 7)), D((pieces, 7)),
+        ],
+        compiler_params=pltpu.CompilerParams(
+            collective_id=2, has_side_effects=True, vmem_limit_bytes=60 << 20
+        ),
+        name="backward",
+    )(da, db, sg, un, wg, wu)
 
 
 def per_device(tokens, out_grads, expert_ids, gates, w_gate, w_up, w_down):
@@ -323,19 +501,8 @@
     blk = jnp.concatenate(
         [jnp.concatenate([meta, meta], axis=0), jnp.concatenate([tokens, out_grads], axis=0)], axis=1
     )
-    gate_mat, up_mat, down_mat = w_gate[0], w_up[0], w_down[0]
-    d_gate, d_up, sg, give = forward(blk, gate_mat, up_mat, down_mat, 4)
-    dots = lax.psum(sg[:, 0], "dp")
-    fisher = (jnp.sum((sg[:, 1] * dots) ** 2) * (1.0 / 256.0)).reshape(1)
-    summed = (times_transposed(d_gate, gate_mat) + times_transposed(d_up, up_mat)).astype(BF16)
-    back = lax.psum_scatter(summed, "dp", scatter_dimension=0, tiled=True)
-    back = back.reshape(NX, NC, NZ, 2, -1).transpose(0, 2, 1, 3, 4).reshape(64, 2, -1)
-    rows = lax.all_to_all(back, "expert", split_axis=0, concat_axis=0, tiled=True)
-    gv = give[:, :, :32].reshape(NX, NC, NZ, 8, NC, NZ, 2)
-    gv = jnp.einsum("xczrczk->xzcrk", gv.astype(F32)).astype(BF16)
-    gv = lax.all_to_all(gv.reshape(64, 8, 2), "expert", split_axis=0, concat_axis=0, tiled=True)
-    out = jnp.einsum("erk,ekd->rd", gv, rows, preferred_element_type=F32)
-    return (out.astype(BF16), fisher)
+    da, db, sg, un = forward(blk, w_gate[0], w_up[0], w_down[0], FORWARD_PIECES)
+    return backward(da, db, sg, un, w_gate[0], w_up[0], BACKWARD_PIECES)
 
 
 def solution(mesh):

time: 335 us -> 264 us (0.79)
  waiting for transfers between devices: 101 us -> 0 us
  Pallas kernels: 161 us -> 255 us
  matrix products: 20.1 us -> 0 us
  starting transfers between devices: 16.4 us -> 0 us
  between operations: 15.9 us -> 2.41 us
  local copies, waits for them, and re-layouts: 10.1 us -> 2.55 us
  blocking collectives: 7.19 us -> 0 us
    pallas_call x0 -> x1, Pallas kernels: none -> 94.3 us  [backward(): pl.pallas_call(functools.partial(backward_kernel, chunks), out_shape=(jax...]
    reduce_scatter x1 -> x0, waiting for transfers between devices: 63.9 us -> none  [per_device(): back = lax.psum_scatter(summed, 'dp', scatter_dimension=0, tiled=True)]
    all_to_all x2 -> x0, waiting for transfers between devices: 36.7 us -> none  [the longest x1 36.6 us: per_device(): lax.all_to_all(back, 'expert', split_axis=0, concat_axis=0, tiled=True)]
    dot_general x3 -> x0, matrix products: 20.1 us -> none  [the longest x2 19.1 us: times_transposed(): lax.dot_general(left, right, (((1,), (1,)), ((), ())), preferred_element_...]
    all_to_all x2 -> x0, starting transfers between devices: 16.4 us -> none  [the longest x1 10.6 us: per_device(): lax.all_to_all(back, 'expert', split_axis=0, concat_axis=0, tiled=True)]
    psum x1 -> x0, blocking collectives: 7.19 us -> none  [per_device(): dots = lax.psum(sg[:, 0], 'dp')]
    reshape x2 -> x0, local copies, waits for them, and re-layouts: 4.53 us -> none  [the longest x1 3.88 us: per_device(): back.reshape(NX, NC, NZ, 2, -1).transpose(0, 2, 1, 3, 4).reshape(64, 2, -1)]
  transfers between devices with their start and end apart: 3 -> 0, of which waited for: 2 -> 0; matrix products, arithmetic and copies ran while one was open for 3% -> 0% of each run, Pallas kernels for 0% -> 0%
where the time goes in v2:
time: 264 us; the launch traced here: 262 us
  Pallas kernels  255 us (97%)
    pallas_call x1, Pallas kernels, forward(): pl.pallas_call(functools.partial(forward_kernel, chunks), out_shape=(shap...  161 us
    pallas_call x1, Pallas kernels, backward(): pl.pallas_call(functools.partial(backward_kernel, chunks), out_shape=(jax...  94.3 us

profile of v2, /device:TPU:1, one launch (start us, length us, event | category | flops | bytes accessed | tf_op | source)
XLA Modules:
  0.0 261.9 jit_solution(13736163625349070779)
XLA Ops:
  0.6 0.0 copy-start
  0.6 0.8 constant_dynamic-slice_fusion
  1.4 0.1 copy.12
  1.5 0.0 copy-done
  1.5 0.1 constant_dynamic-slice_fusion.1
  1.6 0.1 copy.11
  1.6 0.1 fusion.2
  1.7 1.7 maximum_maximum_fusion.blk
  3.4 160.8 %forward.1 = (bf16[512,256]{1,0:T(8,128)(2,1)}, bf16[512,256]{1,0:T(8,128)(2,1)}, f32[4,8,128]{2,1,0:T(8,128)}, bf16[4,128,128]{2,1,0:T(8,128)(2,1)}) custom-call(bf16[16,7296]{1,0:T(8,128)(2,1)} %maximum_maximum_fusion.blk, bf16[7168,256]{1,0:T(8,128)(2,1)} %bitcast.3, bf16[7168,256]{1,0:T(8,128)(2,1)} %bitcast.5, bf16[256,7168]{1,0:T(8,128)(2,1)} %bitcast.7), custom_call_target="tpu_custom_call" | custom-call | tf_op jit(solution)/shard_map/forward/pallas_call | solution.py:291
  164.2 94.3 %backward.1 = (bf16[8,7168]{1,0:T(8,128)(2,1)}, f32[1]{0:T(128)}) custom-call(bf16[512,256]{1,0:T(8,128)(2,1)} %get-tuple-element.6.da, bf16[512,256]{1,0:T(8,128)(2,1)} %get-tuple-element.7.db, f32[4,8,128]{2,1,0:T(8,128)} %get-tuple-element.8.sg, bf16[4,128,128]{2,1,0:T(8,128)(2,1)} %get-tuple-element.9.un, bf16[7168,256]{1,0:T(8,128)(2,1)} %bitcast.4, ...), custom_call_target="tpu_custom_call" | custom-call | tf_op jit(solution)/shard_map/backward/pallas_call | solution.py:470
  258.6 1.6 copy.15
  (1 shorter events, 0.0 us)
Async XLA Ops:
  0.6 0.9 copy-start

commit v3 on v2

--- a/solution.py
+++ b/solution.py
@@ -10,7 +10,11 @@
 F32, BF16 = jnp.float32, jnp.bfloat16
 NX, NZ, NC, NY = 4, 8, 2, 4
 META = 128
-FORWARD_PIECES, BACKWARD_PIECES = 4, 7
+LATE_TILES = (14, 14, 14)
+EARLY_TILES = (7, 7)
+LEAD = 2
+EARLY_SLOTS = (1, 2, 3, 4, 5, 10, 12)
+BACKWARD_PIECES = 7
 MESH = pl.DeviceIdType.MESH
 
 
@@ -41,8 +45,9 @@
 
 
 def forward_kernel(
-    chunks, blk, wg_hbm, wu_hbm, wd_hbm, da_ref, db_ref, sg_ref, un_ref,
-    G, R, S, wg, wu, wd, acc, lsem, zs, zr, xs, xr, cs, cr, ys, yr,
+    chunks, early, blk, wg_hbm, wu_hbm, wd_hbm, da_ref, db_ref, sg_ref, un_ref,
+    G, H, R, S, wg, wu, wd, acc, lsem, xs, xr, zs, zr, cs, cr, ys, yr,
+    ks, kr, hys, hyr, hzs, hzr, hxs, hxr, hcs, hcr,
 ):
     x, z, c, y = position()
     e = lax.axis_index("expert")
@@ -55,6 +60,8 @@
     dzp, dzm = place(x, zp, c, y), place(x, zm, c, y)
     dyp, dym = place(x, z, c, yp), place(x, z, c, ym)
     dco = place(x, z, co, y)
+    dya, dxa = place(x, z, c, ya), place(xa, z, c, y)
+    wide = early[0][0]
     loads = [
         pltpu.make_async_copy(wg_hbm, wg, lsem.at[0]),
         pltpu.make_async_copy(wu_hbm, wu, lsem.at[1]),
@@ -62,8 +69,9 @@
     ]
     for load in loads:
         load.start()
-    G[x, c, z] = blk[...]
-    meet([dxp, dxm, dzp, dzm, dyp, dym, dco])
+    G[z, x, c] = blk[:, :wide]
+    H[x, c, z, y] = blk[:, wide:]
+    meet([dxp, dxm, dxa, dzp, dzm, dyp, dym, dya, dco])
     sent = []
 
     def go(copy):
@@ -78,71 +86,64 @@
         first = size // 2 // 128 * 128
         return pl.ds(start, first), pl.ds(start + first, size - first)
 
-    def zblock(h, off):
-        return G.at[x, c, lax.rem(z + off + NZ, NZ), :, cols(h)]
-
-    def z_send(h, step):
-        if step < 4:
-            b = zblock(h, -step)
-            go(remote(b, b, zs.at[h, step], zr.at[h, step], dzp))
+    others_x = [(dxp, xm), (dxm, xp), (dxa, xa)]
+    others_y = [(dyp, ym), (dym, yp), (dya, ya)]
+    near = [0, -1, 1, -2, 2, -3, 3, 4]
+    phases = [(0,), (1, 2), (3, 4), (5, 6), (7,)]
+
+    def turn(off):
+        return lax.rem(z + off + NZ, NZ)
+
+    def ring(block, step, arriving):
         if step < 3:
-            b = zblock(h, step)
-            go(remote(b, b, zs.at[h, 4 + step], zr.at[h, 4 + step], dzm))
-
-    def z_recv(h, step):
-        if step < 4:
-            b = zblock(h, -step - 1)
-            remote(b, b, zs.at[h, step], zr.at[h, step], dzp).wait_recv()
+            return [
+                (block(-step - arriving, pl.ds(0, 4)), step, dzp),
+                (block(step + arriving, pl.ds(0, 4)), 3 + step, dzm),
+            ]
+        return [
+            (block(-step - arriving, pl.ds(0, 2)), 6, dzp),
+            (block(step + arriving, pl.ds(2, 2)), 7, dzm),
+        ]
+
+    def ring_send(block, send, recv, step):
+        for b, i, device in ring(block, step, 0):
+            go(remote(b, b, send(i), recv(i), device))
+
+    def ring_wait(block, send, recv, step):
+        for b, i, device in ring(block, step, 1):
+            remote(b, b, send(i), recv(i), device).wait_recv()
+
+    def late_x(h):
+        b = G.at[z, x, c, :, cols(h)]
+        for i, (device, _) in enumerate(others_x):
+            go(remote(b, b, xs.at[h, i], xr.at[h, i], device))
+
+    def late_block(h):
+        return lambda off, part: G.at[turn(off), part, c, :, cols(h)]
+
+    def late_share(h, i):
+        b = G.at[turn(near[i]), :, c, :, cols(h)]
+        go(remote(b, b, cs.at[h, i], cr.at[h, i], dco))
+
+    def late_z(h):
+        for i, (device, who) in enumerate(others_x):
+            b = G.at[z, who, c, :, cols(h)]
+            remote(b, b, xs.at[h, i], xr.at[h, i], device).wait_recv()
+        ring_send(late_block(h), lambda i: zs.at[h, i], lambda i: zr.at[h, i], 0)
+        late_share(h, 0)
+
+    def late_advance(h, step):
+        args = (late_block(h), lambda i: zs.at[h, i], lambda i: zr.at[h, i])
+        ring_wait(*args, step)
         if step < 3:
-            b = zblock(h, step + 1)
-            remote(b, b, zs.at[h, 4 + step], zr.at[h, 4 + step], dzm).wait_recv()
-
-    def z_advance(h, step):
-        z_recv(h, step)
-        if step < 3:
-            z_send(h, step + 1)
-
-    def line(h, xx, cc):
-        return G.at[xx, cc, :, :, cols(h)]
-
-    def part(xx, ds):
-        return G.at[xx, c, :, :, ds]
-
-    def share(h, k, xx):
-        b = line(h, xx, c)
-        go(remote(b, b, cs.at[h, k], cr.at[h, k], dco))
-
-    def shared(h, k, xx):
-        b = line(h, xx, co)
-        remote(b, b, cs.at[h, k], cr.at[h, k], dco).wait_recv()
-
-    def x_start(h):
-        b = line(h, x, c)
-        go(remote(b, b, xs.at[h, 0], xr.at[h, 0], dxp))
-        go(remote(b, b, xs.at[h, 1], xr.at[h, 1], dxm))
-        share(h, 0, x)
-
-    def x_forward(h):
-        lo, hi = halves(h)
-        b = line(h, xm, c)
-        remote(b, b, xs.at[h, 0], xr.at[h, 0], dxp).wait_recv()
-        go(remote(part(xm, lo), part(xm, lo), xs.at[h, 2], xr.at[h, 2], dxp))
-        share(h, 1, xm)
-        b = line(h, xp, c)
-        remote(b, b, xs.at[h, 1], xr.at[h, 1], dxm).wait_recv()
-        go(remote(part(xp, hi), part(xp, hi), xs.at[h, 3], xr.at[h, 3], dxm))
-        share(h, 2, xp)
-
-    def x_last(h):
-        lo, hi = halves(h)
-        remote(part(xa, lo), part(xa, lo), xs.at[h, 2], xr.at[h, 2], dxp).wait_recv()
-        remote(part(xa, hi), part(xa, hi), xs.at[h, 3], xr.at[h, 3], dxm).wait_recv()
-        share(h, 3, xa)
-
-    rows = NC * NZ * 16
-
-    def routes(xx):
-        meta = G[xx, :, :, :, 0:META].reshape(rows, META).astype(F32)
+            ring_send(*args, step + 1)
+        for i in phases[step + 1]:
+            late_share(h, i)
+
+    rows = NX * NC * 16
+
+    def routes(zz):
+        meta = G[zz, :, :, :, 0:META].reshape(rows, META).astype(F32)
         lane = lax.broadcasted_iota(jnp.int32, (rows, META), 1)
         chosen = jnp.where(lane < 8, meta, -1.0) == e.astype(F32)
         gates = pltpu.roll(meta, META - 8, 1)
@@ -153,115 +154,182 @@
         earlier = jnp.where((r // 8 == q // 8) & (q < r), 1.0, 0.0).astype(BF16)
         hits = jnp.broadcast_to(hit, (rows, META))
         rank = jnp.dot(earlier, hits.astype(BF16), preferred_element_type=F32)
-        r = lax.broadcasted_iota(jnp.int32, (rows, META), 0)
-        base = (r // 8 % 2) * 32 + (r // 128) * 16 + (r // 16 % 8) * 2
-        match = (lane.astype(F32) == base.astype(F32) + rank) & (hits > 0.5)
-        pick = jnp.where(match, 1.0, 0.0)
-        S[xx] = jnp.transpose(pick)[:64].astype(BF16)
+        slot = (r // 16 * 2).astype(F32) + rank
+        lanes = lane.astype(F32)
+        match = (lanes == slot + (r // 8 % 2 * 16).astype(F32)) & (hits > 0.5)
+        S[y, zz] = jnp.transpose(jnp.where(match, 1.0, 0.0))[:32].astype(BF16)
+        match = (lanes == slot + zz.astype(F32) * 16.0) & (hits > 0.5)
         give = jnp.where(match, jnp.broadcast_to(gate, (rows, META)), 0.0)
-        un_ref[xx] = give.reshape(16, 16, META)[:, :8].reshape(128, META).astype(BF16)
-
-    def pack(h, xx):
+        un_ref[:, :, zz] = give.reshape(NX, NC, 16, META)[:, :, :8]
+
+    def late_pack(h, i):
+        zz = turn(near[i])
+        b = G.at[zz, :, co, :, cols(h)]
+        remote(b, b, cs.at[h, i], cr.at[h, i], dco).wait_recv()
         if h == 0:
-            routes(xx)
-        slab = G[xx, :, :, :, cols(h)].reshape(rows, chunks[h][1])
-        got = jnp.dot(S[xx], slab, preferred_element_type=F32).astype(BF16)
-        R[y, xx, :, :, cols(h)] = got.reshape(2, 32, chunks[h][1])
-
-    def packed(g, xx, ds):
-        return R.at[g, xx, :, :, ds]
-
-    def y_send(h, k, xx):
-        b = packed(y, xx, cols(h))
-        go(remote(b, b, ys.at[h, k, 0], yr.at[h, k, 0], dyp))
-        go(remote(b, b, ys.at[h, k, 1], yr.at[h, k, 1], dym))
-
-    def y_forward(h, k, xx):
+            routes(zz)
+        size = chunks[h][1]
+        slab = G[zz, :, :, :, cols(h)].reshape(rows, size)
+        got = jnp.dot(S[y, zz], slab, preferred_element_type=F32).astype(BF16)
+        R[y, zz, :, :, cols(h)] = got.reshape(2, 16, size)
+        b = R.at[y, zz, :, :, cols(h)]
+        go(remote(b, b, ys.at[h, i, 0], yr.at[h, i, 0], dyp))
+        go(remote(b, b, ys.at[h, i, 1], yr.at[h, i, 1], dym))
+
+    def y_forward(h, i):
+        zz = turn(near[i])
         lo, hi = halves(h)
-        b = packed(ym, xx, cols(h))
-        remote(b, b, ys.at[h, k, 0], yr.at[h, k, 0], dyp).wait_recv()
-        b = packed(ym, xx, lo)
-        go(remote(b, b, ys.at[h, k, 2], yr.at[h, k, 2], dyp))
-        b = packed(yp, xx, cols(h))
-        remote(b, b, ys.at[h, k, 1], yr.at[h, k, 1], dym).wait_recv()
-        b = packed(yp, xx, hi)
-        go(remote(b, b, ys.at[h, k, 3], yr.at[h, k, 3], dym))
-
-    def y_last(h, k, xx):
+        b = R.at[ym, zz, :, :, cols(h)]
+        remote(b, b, ys.at[h, i, 0], yr.at[h, i, 0], dyp).wait_recv()
+        b = R.at[ym, zz, :, :, lo]
+        go(remote(b, b, ys.at[h, i, 2], yr.at[h, i, 2], dyp))
+        b = R.at[yp, zz, :, :, cols(h)]
+        remote(b, b, ys.at[h, i, 1], yr.at[h, i, 1], dym).wait_recv()
+        b = R.at[yp, zz, :, :, hi]
+        go(remote(b, b, ys.at[h, i, 3], yr.at[h, i, 3], dym))
+
+    def y_last(h):
         lo, hi = halves(h)
-        b = packed(ya, xx, lo)
-        remote(b, b, ys.at[h, k, 2], yr.at[h, k, 2], dyp).wait_recv()
-        b = packed(ya, xx, hi)
-        remote(b, b, ys.at[h, k, 3], yr.at[h, k, 3], dym).wait_recv()
-
-    order = [x, xm, xp, xa]
-
-    def multiply(h):
-        start, size = chunks[h]
-        if h == 0:
+        for i in range(NZ):
+            zz = turn(near[i])
+            b = R.at[ya, zz, :, :, lo]
+            remote(b, b, ys.at[h, i, 2], yr.at[h, i, 2], dyp).wait_recv()
+            b = R.at[ya, zz, :, :, hi]
+            remote(b, b, ys.at[h, i, 3], yr.at[h, i, 3], dym).wait_recv()
+
+    def multiply(start, size):
+        if start == 0:
             start, size = META, size - META
             for load in loads:
                 load.wait()
+            acc[...] = jnp.zeros_like(acc)
         f = pl.ds(start - META, size)
         at = pl.ds(start, size)
         tok = R[:, :, 0, :, at].reshape(512, size)
         grad = R[:, :, 1, :, at].reshape(512, size)
-        a = jnp.dot(tok, wg[f, :], preferred_element_type=F32)
-        b = jnp.dot(tok, wu[f, :], preferred_element_type=F32)
-        u = dot_nt(grad, wd[:, f])
-        if h == 0:
-            acc[0], acc[1], acc[2] = a, b, u
+        acc[0] += jnp.dot(tok, wg[f, :], preferred_element_type=F32)
+        acc[1] += jnp.dot(tok, wu[f, :], preferred_element_type=F32)
+        acc[2] += dot_nt(grad, wd[:, f])
+
+    def own(q):
+        return pl.ds(early[q][0] - wide, early[q][1])
+
+    def early_y(q):
+        b = H.at[x, c, z, y, :, own(q)]
+        for i, (device, _) in enumerate(others_y):
+            go(remote(b, b, hys.at[q, i], hyr.at[q, i], device))
+
+    def early_block(q):
+        return lambda off, part: H.at[x, c, turn(off), part, :, own(q)]
+
+    def early_z(q):
+        for i, (device, who) in enumerate(others_y):
+            b = H.at[x, c, z, who, :, own(q)]
+            remote(b, b, hys.at[q, i], hyr.at[q, i], device).wait_recv()
+        ring_send(early_block(q), lambda i: hzs.at[q, i], lambda i: hzr.at[q, i], 0)
+
+    def early_advance(q, step):
+        args = (early_block(q), lambda i: hzs.at[q, i], lambda i: hzr.at[q, i])
+        ring_wait(*args, step)
+        if step < 3:
+            ring_send(*args, step + 1)
         else:
-            acc[0] += a
-            acc[1] += b
-            acc[2] += u
-
-    z_send(0, 0)
-    for step in range(4):
-        z_advance(0, step)
-    x_start(0)
-    waiting = []
+            b = early_line(q, x, c)
+            go(remote(b, b, hxs.at[q, 0], hxr.at[q, 0], dxp))
+            go(remote(b, b, hxs.at[q, 1], hxr.at[q, 1], dxm))
+            early_share(q, 0, x)
+
+    def early_line(q, xx, cc, part=slice(None)):
+        return H.at[xx, cc, part, :, :, own(q)]
+
+    def early_share(q, i, xx):
+        b = early_line(q, xx, c)
+        go(remote(b, b, hcs.at[q, i], hcr.at[q, i], dco))
+
+    def early_forward(q):
+        for i, who, part, device in ((0, xm, pl.ds(0, 4), dxp), (1, xp, pl.ds(4, 4), dxm)):
+            b = early_line(q, who, c)
+            remote(b, b, hxs.at[q, i], hxr.at[q, i], device).wait_recv()
+            b = early_line(q, who, c, part)
+            go(remote(b, b, hxs.at[q, 2 + i], hxr.at[q, 2 + i], device))
+            early_share(q, 1 + i, who)
+
+    def early_last(q):
+        for i, part, device in ((2, pl.ds(0, 4), dxp), (3, pl.ds(4, 4), dxm)):
+            b = early_line(q, xa, c, part)
+            remote(b, b, hxs.at[q, i], hxr.at[q, i], device).wait_recv()
+        early_share(q, 3, xa)
+
+    def early_pack(q):
+        for i, who in enumerate((x, xm, xp, xa)):
+            b = early_line(q, who, co)
+            remote(b, b, hcs.at[q, i], hcr.at[q, i], dco).wait_recv()
+        start, size = early[q]
+
+        def body(i, carry):
+            g, zz = lax.div(i, NZ), lax.rem(i, NZ)
+            slab = H[:, :, zz, g, :, own(q)].reshape(rows, size)
+            got = jnp.dot(S[g, zz], slab, preferred_element_type=F32).astype(BF16)
+            R[g, zz, :, :, pl.ds(start, size)] = got.reshape(2, 16, size)
+            return carry
+
+        lax.fori_loop(0, NY * NZ, body, 0)
+
+    nq = len(early)
+    todo = [[functools.partial(early_z, q) for q in range(nq)]]
+    todo += [[functools.partial(early_advance, q, step) for q in range(nq)] for step in range(4)]
+    todo += [[functools.partial(early_forward, q)] for q in range(nq)]
+    slots = list(EARLY_SLOTS)
+
+    late_x(0)
+    for q in range(nq):
+        early_y(q)
+    for h in range(1, nc):
+        late_x(h)
+    late_z(0)
+    ahead = []
     for h in range(nc):
-        more = h + 1 < nc
-        if more:
-            z_send(h + 1, 0)
-        shared(h, 0, x)
-        pack(h, x)
-        y_send(h, 0, x)
-        if waiting:
-            y_forward(*waiting.pop(0))
-        if more:
-            z_advance(h + 1, 0)
-        x_forward(h)
-        if more:
-            z_advance(h + 1, 1)
-        shared(h, 1, xm)
-        pack(h, xm)
-        y_send(h, 1, xm)
-        y_forward(h, 0, x)
-        if more:
-            z_advance(h + 1, 2)
-        shared(h, 2, xp)
-        pack(h, xp)
-        y_send(h, 2, xp)
-        if more:
-            z_advance(h + 1, 3)
-            x_start(h + 1)
-        x_last(h)
-        y_forward(h, 1, xm)
-        shared(h, 3, xa)
-        pack(h, xa)
-        y_send(h, 3, xa)
-        y_forward(h, 2, xp)
-        waiting.append((h, 3, xa))
-        if h:
-            for k, xx in enumerate(order):
-                y_last(h - 1, k, xx)
-            multiply(h - 1)
-    y_forward(*waiting.pop(0))
-    for k, xx in enumerate(order):
-        y_last(nc - 1, k, xx)
-    multiply(nc - 1)
+        for step in range(-1, 4):
+            ahead.append((max(0, 5 * h + step + 1 - (LEAD if h else 0)), h, step))
+    ahead = [item for item in ahead if item[1:] != (0, -1)]
+    ready = []
+    for slot in range(5 * nc):
+        h, p = divmod(slot, 5)
+        while ahead and ahead[0][0] <= slot:
+            _, hh, step = ahead.pop(0)
+            if step < 0:
+                late_z(hh)
+            else:
+                late_advance(hh, step)
+        for i in phases[p]:
+            late_pack(h, i)
+        while ready:
+            y_forward(*ready.pop(0))
+        ready = [(h, i) for i in phases[p]]
+        if slot == 4:
+            for i, (device, _) in enumerate(others_y):
+                go(remote(S.at[y], S.at[y], ks.at[i], kr.at[i], device))
+        while slots and slots[0] <= slot:
+            slots.pop(0)
+            for event in todo.pop(0):
+                event()
+        if h and p == 2:
+            y_last(h - 1)
+            multiply(*chunks[h - 1])
+    while ready:
+        y_forward(*ready.pop(0))
+    while todo:
+        for event in todo.pop(0):
+            event()
+    for q in range(nq):
+        early_last(q)
+    for i, (device, who) in enumerate(others_y):
+        remote(S.at[who], S.at[who], ks.at[i], kr.at[i], device).wait_recv()
+    for q in range(nq):
+        early_pack(q)
+        multiply(*early[q])
+    y_last(nc - 1)
+    multiply(*chunks[nc - 1])
     lane = lax.broadcasted_iota(jnp.int32, (128, META), 1)
     for g in range(4):
         at = pl.ds(g * 128, 128)
@@ -279,31 +347,39 @@
         copy.wait_send()
 
 
-def forward(blk, wg, wu, wd, pieces):
+def forward(blk, wg, wu, wd):
     width = blk.shape[1] - META
-    step = width // pieces
-    chunks = [(META + i * step, step) for i in range(pieces)]
-    chunks[0] = (0, META + step)
+    chunks, start = [], 0
+    for tiles in LATE_TILES + EARLY_TILES:
+        size = tiles * 128 + (0 if start else META)
+        chunks.append((start, size))
+        start += size
+    pieces, nq = len(LATE_TILES), len(EARLY_TILES)
+    chunks, early = chunks[:pieces], chunks[pieces:]
+    wide = early[0][0]
     vm = pl.BlockSpec(memory_space=pltpu.VMEM)
     hbm = pl.BlockSpec(memory_space=pl.ANY)
     D = pltpu.SemaphoreType.DMA
     shape = jax.ShapeDtypeStruct
     return pl.pallas_call(
-        functools.partial(forward_kernel, chunks),
+        functools.partial(forward_kernel, chunks, early),
         out_shape=(
             shape((512, 256), BF16), shape((512, 256), BF16), shape((NY, 8, META), F32),
-            shape((NX, 128, META), BF16),
+            shape((NX, NC, NZ, 8, META), F32),
         ),
         in_specs=[vm, hbm, hbm, hbm],
         out_specs=(vm, vm, vm, vm),
         scratch_shapes=[
-            pltpu.VMEM((NX, NC, NZ, 16, width + META), BF16),
-            pltpu.VMEM((NY, NX, 2, 32, width + META), BF16),
-            pltpu.VMEM((NX, 64, 256), BF16),
+            pltpu.VMEM((NZ, NX, NC, 16, wide), BF16),
+            pltpu.VMEM((NX, NC, NZ, NY, 16, width + META - wide), BF16),
+            pltpu.VMEM((NY, NZ, 2, 16, width + META), BF16),
+            pltpu.VMEM((NY, NZ, 32, 128), BF16),
             pltpu.VMEM((width, 256), BF16), pltpu.VMEM((width, 256), BF16), pltpu.VMEM((256, width), BF16),
             pltpu.VMEM((3, 512, 256), F32),
-            D((3,)), D((pieces, 7)), D((pieces, 7)), D((pieces, 4)), D((pieces, 4)),
-            D((pieces, 4)), D((pieces, 4)), D((pieces, 4, 4)), D((pieces, 4, 4)),
+            D((3,)), D((pieces, 3)), D((pieces, 3)), D((pieces, 8)), D((pieces, 8)),
+            D((pieces, 8)), D((pieces, 8)), D((pieces, 8, 4)), D((pieces, 8, 4)),
+            D((3,)), D((3,)), D((nq, 3)), D((nq, 3)), D((nq, 8)), D((nq, 8)),
+            D((nq, 4)), D((nq, 4)), D((nq, 4)), D((nq, 4)),
         ],
         compiler_params=pltpu.CompilerParams(
             collective_id=1, has_side_effects=True, vmem_limit_bytes=60 << 20
@@ -368,29 +444,29 @@
         loads[2 * h].wait()
         loads[2 * h + 1].wait()
         part = dot_nt(da[...], wg[at, :]) + dot_nt(db[...], wu[at, :])
-        O[:, :, :, at] = part.astype(BF16).reshape(NY, NX, 32, chunks[h][1])
+        O[:, :, at] = part.astype(BF16).reshape(NY, 128, chunks[h][1])
         lo, hi = halves(h)
-        go(remote(O.at[ya, :, :, lo], R1.at[0, :, :, half(h)], ys.at[h, 0], yr.at[h, 0], dyp))
-        go(remote(O.at[ya, :, :, hi], R1.at[1, :, :, half(h)], ys.at[h, 1], yr.at[h, 1], dym))
+        go(remote(O.at[ya, :, lo], R1.at[0, :, half(h)], ys.at[h, 0], yr.at[h, 0], dyp))
+        go(remote(O.at[ya, :, hi], R1.at[1, :, half(h)], ys.at[h, 1], yr.at[h, 1], dym))
 
     def stage_b(h):
         at = rows_of(h)
         lo, hi = halves(h)
-        got(R1.at[0, :, :, half(h)], ys.at[h, 0], yr.at[h, 0], dyp)
-        O[yp, :, :, lo] = (up(O[yp, :, :, lo]) + up(R1[0, :, :, half(h)])).astype(BF16)
-        go(remote(O.at[yp, :, :, at], R2.at[0, :, :, at], ys.at[h, 2], yr.at[h, 2], dyp))
-        got(R1.at[1, :, :, half(h)], ys.at[h, 1], yr.at[h, 1], dym)
-        O[ym, :, :, hi] = (up(O[ym, :, :, hi]) + up(R1[1, :, :, half(h)])).astype(BF16)
-        go(remote(O.at[ym, :, :, at], R2.at[1, :, :, at], ys.at[h, 3], yr.at[h, 3], dym))
+        got(R1.at[0, :, half(h)], ys.at[h, 0], yr.at[h, 0], dyp)
+        O[yp, :, lo] = (up(O[yp, :, lo]) + up(R1[0, :, half(h)])).astype(BF16)
+        go(remote(O.at[yp, :, at], R2.at[0, :, at], ys.at[h, 2], yr.at[h, 2], dyp))
+        got(R1.at[1, :, half(h)], ys.at[h, 1], yr.at[h, 1], dym)
+        O[ym, :, hi] = (up(O[ym, :, hi]) + up(R1[1, :, half(h)])).astype(BF16)
+        go(remote(O.at[ym, :, at], R2.at[1, :, at], ys.at[h, 3], yr.at[h, 3], dym))
 
     def stage_c(h):
         at = rows_of(h)
-        got(R2.at[0, :, :, at], ys.at[h, 2], yr.at[h, 2], dyp)
-        got(R2.at[1, :, :, at], ys.at[h, 3], yr.at[h, 3], dym)
+        got(R2.at[0, :, at], ys.at[h, 2], yr.at[h, 2], dyp)
+        got(R2.at[1, :, at], ys.at[h, 3], yr.at[h, 3], dym)
+        back = (up(O[y, :, at]) + up(R2[0, :, at]) + up(R2[1, :, at])).astype(BF16)
         for t in range(NX):
-            back = (up(O[y, t, :, at]) + up(R2[0, t, :, at]) + up(R2[1, t, :, at])).astype(BF16)
-            mine = un[t, pl.ds(pl.multiple_of(c * 64, 64), 64), :][:, :32]
-            theirs = un[t, pl.ds(pl.multiple_of(co * 64, 64), 64), :][:, :32]
+            mine = un[t, c].reshape(64, META).astype(BF16)
+            theirs = un[t, co].reshape(64, META).astype(BF16)
             DS[t, :, at] = jnp.dot(theirs, back, preferred_element_type=F32).astype(BF16)
             E[t, :, at] = jnp.dot(mine, back, preferred_element_type=F32).astype(BF16)
         go(remote(DS.at[:, :, at], RC.at[:, :, at], cs.at[h], cr.at[h], dco))
@@ -473,9 +549,9 @@
         in_specs=[vm, vm, vm, vm, hbm, hbm],
         out_specs=(vm, pl.BlockSpec(memory_space=pltpu.SMEM)),
         scratch_shapes=[
-            pltpu.VMEM((NY, NX, 32, width), BF16),
-            pltpu.VMEM((2, NX, 32, width // 2), BF16),
-            pltpu.VMEM((2, NX, 32, width), BF16),
+            pltpu.VMEM((NY, 128, width), BF16),
+            pltpu.VMEM((2, 128, width // 2), BF16),
+            pltpu.VMEM((2, 128, width), BF16),
             pltpu.VMEM((NX, 64, width), BF16), pltpu.VMEM((NX, 64, width), BF16), pltpu.VMEM((NX, 64, width), BF16),
             pltpu.VMEM((2, 64, width // 2), BF16),
             pltpu.VMEM((2, 64, width), BF16),
@@ -501,7 +577,7 @@
     blk = jnp.concatenate(
         [jnp.concatenate([meta, meta], axis=0), jnp.concatenate([tokens, out_grads], axis=0)], axis=1
     )
-    da, db, sg, un = forward(blk, w_gate[0], w_up[0], w_down[0], FORWARD_PIECES)
+    da, db, sg, un = forward(blk, w_gate[0], w_up[0], w_down[0])
     return backward(da, db, sg, un, w_gate[0], w_up[0], BACKWARD_PIECES)
 
 

time: 264 us -> 251 us (0.951)
  Pallas kernels: 255 us -> 242 us
    pallas_call x1, Pallas kernels: 161 us -> 149 us  [forward(): pl.pallas_call(functools.partial(forward_kernel, chunks, early), out_shap...]
where the time goes in v3:
time: 251 us; the launch traced here: 249 us
  Pallas kernels  242 us (96%)
  local copies, waits for them, and re-layouts  2.55 us (1%)
    pallas_call x1, Pallas kernels, forward(): pl.pallas_call(functools.partial(forward_kernel, chunks, early), out_shap...  149 us
    pallas_call x1, Pallas kernels, backward(): pl.pallas_call(functools.partial(backward_kernel, chunks), out_shape=(jax...  92.7 us

profile of v3, /device:TPU:1, one launch (start us, length us, event | category | flops | bytes accessed | tf_op | source)
XLA Modules:
  0.0 248.7 jit_solution(7474546671533807811)
XLA Ops:
  0.6 0.0 copy-start
  0.6 0.8 constant_dynamic-slice_fusion
  1.4 0.1 copy.12
  1.5 0.0 copy-done
  1.5 0.1 constant_dynamic-slice_fusion.1
  1.6 0.1 copy.11
  1.6 0.1 fusion.2
  1.7 1.7 maximum_maximum_fusion.blk
  3.4 149.3 %forward.1 = (bf16[512,256]{1,0:T(8,128)(2,1)}, bf16[512,256]{1,0:T(8,128)(2,1)}, f32[4,8,128]{2,1,0:T(8,128)}, f32[4,2,8,8,128]{4,3,2,1,0:T(8,128)}) custom-call(bf16[16,7296]{1,0:T(8,128)(2,1)} %maximum_maximum_fusion.blk, bf16[7168,256]{1,0:T(8,128)(2,1)} %bitcast.3, bf16[7168,256]{1,0:T(8,128)(2,1)} %bitcast.5, bf16[256,7168]{1,0:T(8,128)(2,1)} %bitcast.7), custom_call_target="tpu_custom_call" | custom-call | tf_op jit(solution)/shard_map/forward/pallas_call | solution.py:364
  152.7 92.7 %backward.1 = (bf16[8,7168]{1,0:T(8,128)(2,1)}, f32[1]{0:T(128)}) custom-call(bf16[512,256]{1,0:T(8,128)(2,1)} %get-tuple-element.6.da, bf16[512,256]{1,0:T(8,128)(2,1)} %get-tuple-element.7.db, f32[4,8,128]{2,1,0:T(8,128)} %get-tuple-element.8.sg, f32[4,2,8,8,128]{4,3,2,1,0:T(8,128)} %get-tuple-element.9.un, bf16[7168,256]{1,0:T(8,128)(2,1)} %bitcast.4, ...), custom_call_target="tpu_custom_call" | custom-call | tf_op jit(solution)/shard_map/backward/pallas_call | solution.py:546
  245.4 1.6 copy.15
  (1 shorter events, 0.0 us)
Async XLA Ops:
  0.6 0.9 copy-start

commit v4 on v3

--- a/solution.py
+++ b/solution.py
@@ -10,11 +10,12 @@
 F32, BF16 = jnp.float32, jnp.bfloat16
 NX, NZ, NC, NY = 4, 8, 2, 4
 META = 128
-LATE_TILES = (14, 14, 14)
-EARLY_TILES = (7, 7)
-LEAD = 2
-EARLY_SLOTS = (1, 2, 3, 4, 5, 10, 12)
-BACKWARD_PIECES = 7
+LATE_TILES = (16, 18, 10)
+EARLY_TILES = (12,)
+LEAD, LAG = 1, 2
+EARLY_SLOTS = (0, 1, 2, 3, 4, 9, 13, 14)
+BACKWARD_TILES = (8,) * 7
+BACKWARD_LAGS = (0, 2, 4, 5, 6, 7)
 MESH = pl.DeviceIdType.MESH
 
 
@@ -125,12 +126,14 @@
         b = G.at[turn(near[i]), :, c, :, cols(h)]
         go(remote(b, b, cs.at[h, i], cr.at[h, i], dco))
 
-    def late_z(h):
+    def late_near(h):
         for i, (device, who) in enumerate(others_x):
             b = G.at[z, who, c, :, cols(h)]
             remote(b, b, xs.at[h, i], xr.at[h, i], device).wait_recv()
+        late_share(h, 0)
+
+    def late_z(h):
         ring_send(late_block(h), lambda i: zs.at[h, i], lambda i: zr.at[h, i], 0)
-        late_share(h, 0)
 
     def late_advance(h, step):
         args = (late_block(h), lambda i: zs.at[h, i], lambda i: zr.at[h, i])
@@ -275,10 +278,19 @@
 
         lax.fori_loop(0, NY * NZ, body, 0)
 
+    def early_finish(q):
+        if q == 0:
+            for i, (device, who) in enumerate(others_y):
+                remote(S.at[who], S.at[who], ks.at[i], kr.at[i], device).wait_recv()
+        early_pack(q)
+        multiply(*early[q])
+
     nq = len(early)
     todo = [[functools.partial(early_z, q) for q in range(nq)]]
     todo += [[functools.partial(early_advance, q, step) for q in range(nq)] for step in range(4)]
     todo += [[functools.partial(early_forward, q)] for q in range(nq)]
+    todo += [[functools.partial(early_last, q)] for q in range(nq)]
+    todo += [[functools.partial(early_finish, q)] for q in range(nq)]
     slots = list(EARLY_SLOTS)
 
     late_x(0)
@@ -286,13 +298,25 @@
         early_y(q)
     for h in range(1, nc):
         late_x(h)
+    while slots and slots[0] < 0:
+        slots.pop(0)
+        for event in todo.pop(0):
+            event()
+    late_near(0)
     late_z(0)
+    for h in range(1, nc):
+        late_near(h)
     ahead = []
     for h in range(nc):
         for step in range(-1, 4):
             ahead.append((max(0, 5 * h + step + 1 - (LEAD if h else 0)), h, step))
     ahead = [item for item in ahead if item[1:] != (0, -1)]
     ready = []
+
+    def forward_until(slot):
+        while ready and ready[0][0] <= slot:
+            y_forward(*ready.pop(0)[1:])
+
     for slot in range(5 * nc):
         h, p = divmod(slot, 5)
         while ahead and ahead[0][0] <= slot:
@@ -301,11 +325,11 @@
                 late_z(hh)
             else:
                 late_advance(hh, step)
-        for i in phases[p]:
-            late_pack(h, i)
-        while ready:
-            y_forward(*ready.pop(0))
-        ready = [(h, i) for i in phases[p]]
+        now = [(hh, 0) for hh in range(nc)] if slot == 0 else [(h, i) for i in phases[p] if i]
+        for item in now:
+            late_pack(*item)
+        forward_until(slot - LAG)
+        ready += [(slot, *item) for item in now]
         if slot == 4:
             for i, (device, _) in enumerate(others_y):
                 go(remote(S.at[y], S.at[y], ks.at[i], kr.at[i], device))
@@ -314,20 +338,13 @@
             for event in todo.pop(0):
                 event()
         if h and p == 2:
+            forward_until(5 * h - 1)
             y_last(h - 1)
             multiply(*chunks[h - 1])
-    while ready:
-        y_forward(*ready.pop(0))
+    forward_until(5 * nc)
     while todo:
         for event in todo.pop(0):
             event()
-    for q in range(nq):
-        early_last(q)
-    for i, (device, who) in enumerate(others_y):
-        remote(S.at[who], S.at[who], ks.at[i], kr.at[i], device).wait_recv()
-    for q in range(nq):
-        early_pack(q)
-        multiply(*early[q])
     y_last(nc - 1)
     multiply(*chunks[nc - 1])
     lane = lax.broadcasted_iota(jnp.int32, (128, META), 1)
@@ -390,17 +407,20 @@
 
 def backward_kernel(
     chunks, da, db, sg, un, wg_hbm, wu_hbm, out_ref, fis_ref,
-    O, R1, R2, E, DS, RC, X1, X2, Fz, RZ, SB, wg, wu,
+    O, R1, R2, E, DS, RC, X, Fz, RZ, SB, wg, wu,
     lsem, ss, sr, ys, yr, cs, cr, xs, xr, zs, zr,
 ):
     x, z, c, y = position()
     nc = len(chunks)
     xp, xm, xa = lax.rem(x + 1, NX), lax.rem(x + NX - 1, NX), lax.rem(x + 2, NX)
-    zp, zm = lax.rem(z + 1, NZ), lax.rem(z + NZ - 1, NZ)
     yp, ym, ya = lax.rem(y + 1, NY), lax.rem(y + NY - 1, NY), lax.rem(y + 2, NY)
     co = 1 - c
-    dxp, dxm = place(xp, z, c, y), place(xm, z, c, y)
-    dzp, dzm = place(x, zp, c, y), place(x, zm, c, y)
+    dxp, dxm, dxa = place(xp, z, c, y), place(xm, z, c, y), place(xa, z, c, y)
+    reach = (1, -1, 2, -2, 3, -3, 4)
+
+    def turn(off):
+        return lax.rem(z + off + NZ, NZ)
+
     dyp, dym, dya = place(x, z, c, yp), place(x, z, c, ym), place(x, z, c, ya)
     dco = place(x, z, co, y)
 
@@ -414,7 +434,7 @@
             load.start()
             loads.append(load)
     SB[y] = sg[...]
-    meet([dxp, dxm, dzp, dzm, dyp, dym, dya, dco])
+    meet([dxp, dxm, dxa, dyp, dym, dya, dco] + [place(x, turn(off), c, y) for off in reach])
     sent = []
 
     def go(copy):
@@ -473,59 +493,37 @@
 
     def stage_d(h):
         at = rows_of(h)
-        lo, hi = halves(h)
         got(RC.at[:, :, at], cs.at[h], cr.at[h], dco)
         E[:, :, at] = (up(E[:, :, at]) + up(RC[:, :, at])).astype(BF16)
-        go(remote(E.at[xa, :, lo], X1.at[0, :, half(h)], xs.at[h, 0], xr.at[h, 0], dxp))
-        go(remote(E.at[xa, :, hi], X1.at[1, :, half(h)], xs.at[h, 1], xr.at[h, 1], dxm))
+        for i, (who, device) in enumerate(((xp, dxp), (xm, dxm), (xa, dxa))):
+            go(remote(E.at[who, :, at], X.at[i, :, at], xs.at[h, i], xr.at[h, i], device))
 
     def stage_e(h):
         at = rows_of(h)
+        total = up(E[x, :, at])
+        for i in range(3):
+            got(X.at[i, :, at], xs.at[h, i], xr.at[h, i], dxp)
+            total += up(X[i, :, at])
+        size = chunks[h][1]
+        total = total.reshape(NZ, 8, size)
+        total = jnp.concatenate([total[:, :, : size // 2], total[:, :, size // 2 :]], axis=1)
+        Fz[:, :, half(h)] = total.astype(BF16)
+        for i, off in enumerate(reach):
+            src = Fz.at[turn(off), :, half(h)]
+            go(remote(src, RZ.at[i, :, half(h)], zs.at[h, i], zr.at[h, i], place(x, turn(off), c, y)))
+
+    def stage_f(h):
         lo, hi = halves(h)
-        got(X1.at[0, :, half(h)], xs.at[h, 0], xr.at[h, 0], dxp)
-        E[xp, :, lo] = (up(E[xp, :, lo]) + up(X1[0, :, half(h)])).astype(BF16)
-        go(remote(E.at[xp, :, at], X2.at[0, :, at], xs.at[h, 2], xr.at[h, 2], dxp))
-        got(X1.at[1, :, half(h)], xs.at[h, 1], xr.at[h, 1], dxm)
-        E[xm, :, hi] = (up(E[xm, :, hi]) + up(X1[1, :, half(h)])).astype(BF16)
-        go(remote(E.at[xm, :, at], X2.at[1, :, at], xs.at[h, 3], xr.at[h, 3], dxm))
-
-    def zrow(off):
-        return lax.rem(z + off + NZ, NZ)
-
-    def z_send(h, step):
-        at = rows_of(h)
-        if step < 4:
-            go(remote(Fz.at[zrow(4 - step), :, at], RZ.at[step, :, at], zs.at[h, step], zr.at[h, step], dzp))
-        if step < 3:
-            go(remote(Fz.at[zrow(step - 3), :, at], RZ.at[4 + step, :, at], zs.at[h, 4 + step], zr.at[h, 4 + step], dzm))
-
-    def stage_f(h):
-        at = rows_of(h)
-        got(X2.at[0, :, at], xs.at[h, 2], xr.at[h, 2], dxp)
-        got(X2.at[1, :, at], xs.at[h, 3], xr.at[h, 3], dxm)
-        total = up(E[x, :, at]) + up(X2[0, :, at]) + up(X2[1, :, at])
-        Fz[:, :, at] = total.reshape(NZ, 8, chunks[h][1])
-        z_send(h, 0)
-
-    def stage_z(step):
-        def run(h):
-            at = rows_of(h)
-            got(RZ.at[step - 1, :, at], zs.at[h, step - 1], zr.at[h, step - 1], dzp)
-            Fz[zrow(4 - step), :, at] += RZ[step - 1, :, at]
-            if step < 4:
-                got(RZ.at[3 + step, :, at], zs.at[h, 3 + step], zr.at[h, 3 + step], dzm)
-                Fz[zrow(step - 3), :, at] += RZ[3 + step, :, at]
-                if step < 3:
-                    z_send(h, step)
-                else:
-                    go(remote(Fz.at[zrow(1), :, at], RZ.at[3, :, at], zs.at[h, 3], zr.at[h, 3], dzp))
-            else:
-                out_ref[:, at] = Fz[z, :, at].astype(BF16)
-        return run
-
-    stages = [stage_a, stage_b, stage_c, stage_d, stage_e, stage_f] + [stage_z(i) for i in (1, 2, 3, 4)]
-    for i in range(nc + len(stages) - 1):
-        for lag, stage in enumerate(stages):
+        total = up(Fz[z, :, half(h)])
+        for i in range(7):
+            got(RZ.at[i, :, half(h)], zs.at[h, i], zr.at[h, i], dxp)
+            total += up(RZ[i, :, half(h)])
+        out_ref[:, lo] = total[:8].astype(BF16)
+        out_ref[:, hi] = total[8:].astype(BF16)
+
+    stages = [stage_a, stage_b, stage_c, stage_d, stage_e, stage_f]
+    for i in range(nc + BACKWARD_LAGS[-1]):
+        for lag, stage in zip(BACKWARD_LAGS, stages):
             if 0 <= i - lag < nc:
                 stage(i - lag)
     for i, (device, who) in enumerate(score):
@@ -536,10 +534,13 @@
         copy.wait_send()
 
 
-def backward(da, db, sg, un, wg, wu, pieces):
+def backward(da, db, sg, un, wg, wu):
     width = wg.shape[0]
-    step = width // pieces
-    chunks = [(i * step, step) for i in range(pieces)]
+    chunks, start = [], 0
+    for tiles in BACKWARD_TILES:
+        chunks.append((start, tiles * 128))
+        start += tiles * 128
+    pieces = len(chunks)
     vm = pl.BlockSpec(memory_space=pltpu.VMEM)
     hbm = pl.BlockSpec(memory_space=pl.ANY)
     D = pltpu.SemaphoreType.DMA
@@ -553,14 +554,13 @@
             pltpu.VMEM((2, 128, width // 2), BF16),
             pltpu.VMEM((2, 128, width), BF16),
             pltpu.VMEM((NX, 64, width), BF16), pltpu.VMEM((NX, 64, width), BF16), pltpu.VMEM((NX, 64, width), BF16),
-            pltpu.VMEM((2, 64, width // 2), BF16),
-            pltpu.VMEM((2, 64, width), BF16),
-            pltpu.VMEM((NZ, 8, width), F32),
-            pltpu.VMEM((7, 8, width), F32),
+            pltpu.VMEM((3, 64, width), BF16),
+            pltpu.VMEM((NZ, 16, width // 2), BF16),
+            pltpu.VMEM((7, 16, width // 2), BF16),
             pltpu.VMEM((NY, NY, 8, META), F32),
             pltpu.VMEM((width, 256), BF16), pltpu.VMEM((width, 256), BF16),
             D((pieces, 2)), D((3,)), D((3,)), D((pieces, 4)), D((pieces, 4)), D((pieces,)), D((pieces,)),
-            D((pieces, 4)), D((pieces, 4)), D((pieces, 7)), D((pieces, 7)),
+            D((pieces, 3)), D((pieces, 3)), D((pieces, 7)), D((pieces, 7)),
         ],
         compiler_params=pltpu.CompilerParams(
             collective_id=2, has_side_effects=True, vmem_limit_bytes=60 << 20
@@ -578,7 +578,7 @@
         [jnp.concatenate([meta, meta], axis=0), jnp.concatenate([tokens, out_grads], axis=0)], axis=1
     )
     da, db, sg, un = forward(blk, w_gate[0], w_up[0], w_down[0])
-    return backward(da, db, sg, un, w_gate[0], w_up[0], BACKWARD_PIECES)
+    return backward(da, db, sg, un, w_gate[0], w_up[0])
 
 
 def solution(mesh):

time: 251 us -> 229 us (0.912)
  Pallas kernels: 242 us -> 222 us
    pallas_call x1, Pallas kernels: 149 us -> 135 us  [forward(): pl.pallas_call(functools.partial(forward_kernel, chunks, early), out_shap...]
    pallas_call x1, Pallas kernels: 92.7 us -> 87.6 us  [backward(): pl.pallas_call(functools.partial(backward_kernel, chunks), out_shape=(jax...]
where the time goes in v4:
time: 229 us
  Pallas kernels  222 us (97%)
  local copies, waits for them, and re-layouts  2.55 us (1%)
  between operations  2.43 us (1%)
    pallas_call x1, Pallas kernels, forward(): pl.pallas_call(functools.partial(forward_kernel, chunks, early), out_shap...  135 us
    pallas_call x1, Pallas kernels, backward(): pl.pallas_call(functools.partial(backward_kernel, chunks), out_shape=(jax...  87.6 us

profile of v4, /device:TPU:1, one launch (start us, length us, event | category | flops | bytes accessed | tf_op | source)
XLA Modules:
  0.0 229.0 jit_solution(2349538115693380678)
XLA Ops:
  0.6 0.0 copy-start
  0.6 0.8 constant_dynamic-slice_fusion
  1.4 0.1 copy.12
  1.5 0.0 copy-done
  1.5 0.1 constant_dynamic-slice_fusion.1
  1.6 0.1 copy.11
  1.6 0.1 fusion.2
  1.7 1.7 maximum_maximum_fusion.blk
  3.4 134.7 %forward.1 = (bf16[512,256]{1,0:T(8,128)(2,1)}, bf16[512,256]{1,0:T(8,128)(2,1)}, f32[4,8,128]{2,1,0:T(8,128)}, f32[4,2,8,8,128]{4,3,2,1,0:T(8,128)}) custom-call(bf16[16,7296]{1,0:T(8,128)(2,1)} %maximum_maximum_fusion.blk, bf16[7168,256]{1,0:T(8,128)(2,1)} %bitcast.3, bf16[7168,256]{1,0:T(8,128)(2,1)} %bitcast.5, bf16[256,7168]{1,0:T(8,128)(2,1)} %bitcast.7), custom_call_target="tpu_custom_call" | custom-call | tf_op jit(solution)/shard_map/forward/pallas_call | solution.py:381
  138.1 87.6 %backward.1 = (bf16[8,7168]{1,0:T(8,128)(2,1)}, f32[1]{0:T(128)}) custom-call(bf16[512,256]{1,0:T(8,128)(2,1)} %get-tuple-element.6.da, bf16[512,256]{1,0:T(8,128)(2,1)} %get-tuple-element.7.db, f32[4,8,128]{2,1,0:T(8,128)} %get-tuple-element.8.sg, f32[4,2,8,8,128]{4,3,2,1,0:T(8,128)} %get-tuple-element.9.un, bf16[7168,256]{1,0:T(8,128)(2,1)} %bitcast.4, ...), custom_call_target="tpu_custom_call" | custom-call | tf_op jit(solution)/shard_map/backward/pallas_call | solution.py:547
  225.7 1.6 copy.15
  (1 shorter events, 0.0 us)
Async XLA Ops:
  0.6 0.9 copy-start

commit v5 on v4

--- a/solution.py
+++ b/solution.py
@@ -10,12 +10,14 @@
 F32, BF16 = jnp.float32, jnp.bfloat16
 NX, NZ, NC, NY = 4, 8, 2, 4
 META = 128
-LATE_TILES = (16, 18, 10)
-EARLY_TILES = (12,)
+LATE_TILES = (14, 18, 14)
+EARLY_TILES = (10,)
 LEAD, LAG = 1, 2
-EARLY_SLOTS = (0, 1, 2, 3, 4, 9, 13, 14)
+EARLY_SLOTS = (1, 2, 3, 4, 5, 9, 12, 13, 14, 99)
+MUL = 3
 BACKWARD_TILES = (8,) * 7
-BACKWARD_LAGS = (0, 2, 4, 5, 6, 7)
+BACKWARD_LAGS = (0, 2, 3, 3, 4, 5)
+BACKWARD_ORDER = (1, 2, 3, 4, 5, 0)
 MESH = pl.DeviceIdType.MESH
 
 
@@ -263,10 +265,14 @@
             remote(b, b, hxs.at[q, i], hxr.at[q, i], device).wait_recv()
         early_share(q, 3, xa)
 
-    def early_pack(q):
+    def early_arrived(q):
         for i, who in enumerate((x, xm, xp, xa)):
             b = early_line(q, who, co)
             remote(b, b, hcs.at[q, i], hcr.at[q, i], dco).wait_recv()
+
+    def early_pack(q, some):
+        if some == 0:
+            early_arrived(q)
         start, size = early[q]
 
         def body(i, carry):
@@ -276,21 +282,20 @@
             R[g, zz, :, :, pl.ds(start, size)] = got.reshape(2, 16, size)
             return carry
 
-        lax.fori_loop(0, NY * NZ, body, 0)
-
-    def early_finish(q):
-        if q == 0:
-            for i, (device, who) in enumerate(others_y):
-                remote(S.at[who], S.at[who], ks.at[i], kr.at[i], device).wait_recv()
-        early_pack(q)
-        multiply(*early[q])
+        lax.fori_loop(some * 16, some * 16 + 16, body, 0)
+
+    def picks_arrived():
+        for i, (device, who) in enumerate(others_y):
+            remote(S.at[who], S.at[who], ks.at[i], kr.at[i], device).wait_recv()
 
     nq = len(early)
     todo = [[functools.partial(early_z, q) for q in range(nq)]]
     todo += [[functools.partial(early_advance, q, step) for q in range(nq)] for step in range(4)]
     todo += [[functools.partial(early_forward, q)] for q in range(nq)]
     todo += [[functools.partial(early_last, q)] for q in range(nq)]
-    todo += [[functools.partial(early_finish, q)] for q in range(nq)]
+    todo[-1].append(picks_arrived)
+    todo += [[functools.partial(early_pack, q, some) for q in range(nq)] for some in (0, 1)]
+    todo += [[functools.partial(multiply, *early[q]) for q in range(nq)]]
     slots = list(EARLY_SLOTS)
 
     late_x(0)
@@ -337,7 +342,7 @@
             slots.pop(0)
             for event in todo.pop(0):
                 event()
-        if h and p == 2:
+        if h and p == MUL:
             forward_until(5 * h - 1)
             y_last(h - 1)
             multiply(*chunks[h - 1])
@@ -523,7 +528,8 @@
 
     stages = [stage_a, stage_b, stage_c, stage_d, stage_e, stage_f]
     for i in range(nc + BACKWARD_LAGS[-1]):
-        for lag, stage in zip(BACKWARD_LAGS, stages):
+        for n in BACKWARD_ORDER:
+            lag, stage = BACKWARD_LAGS[n], stages[n]
             if 0 <= i - lag < nc:
                 stage(i - lag)
     for i, (device, who) in enumerate(score):

time: 229 us -> 223 us (0.974)
  Pallas kernels: 222 us -> 216 us
    pallas_call x1, Pallas kernels: 135 us -> 129 us  [forward(): pl.pallas_call(functools.partial(forward_kernel, chunks, early), out_shap...]
where the time goes in v5:
time: 223 us
  Pallas kernels  216 us (97%)
  local copies, waits for them, and re-layouts  2.55 us (1%)
  between operations  2.43 us (1%)
    pallas_call x1, Pallas kernels, forward(): pl.pallas_call(functools.partial(forward_kernel, chunks, early), out_shap...  129 us
    pallas_call x1, Pallas kernels, backward(): pl.pallas_call(functools.partial(backward_kernel, chunks), out_shape=(jax...  86.9 us

profile of v5, /device:TPU:1, one launch (start us, length us, event | category | flops | bytes accessed | tf_op | source)
XLA Modules:
  0.0 222.6 jit_solution(4141274364504801076)
XLA Ops:
  0.6 0.0 copy-start
  0.6 0.8 constant_dynamic-slice_fusion
  1.4 0.1 copy.12
  1.5 0.0 copy-done
  1.5 0.1 constant_dynamic-slice_fusion.1
  1.6 0.1 copy.11
  1.6 0.1 fusion.2
  1.7 1.7 maximum_maximum_fusion.blk
  3.4 129.0 %forward.1 = (bf16[512,256]{1,0:T(8,128)(2,1)}, bf16[512,256]{1,0:T(8,128)(2,1)}, f32[4,8,128]{2,1,0:T(8,128)}, f32[4,2,8,8,128]{4,3,2,1,0:T(8,128)}) custom-call(bf16[16,7296]{1,0:T(8,128)(2,1)} %maximum_maximum_fusion.blk, bf16[7168,256]{1,0:T(8,128)(2,1)} %bitcast.3, bf16[7168,256]{1,0:T(8,128)(2,1)} %bitcast.5, bf16[256,7168]{1,0:T(8,128)(2,1)} %bitcast.7), custom_call_target="tpu_custom_call" | custom-call | tf_op jit(solution)/shard_map/forward/pallas_call | solution.py:386
  132.4 86.9 %backward.1 = (bf16[8,7168]{1,0:T(8,128)(2,1)}, f32[1]{0:T(128)}) custom-call(bf16[512,256]{1,0:T(8,128)(2,1)} %get-tuple-element.6.da, bf16[512,256]{1,0:T(8,128)(2,1)} %get-tuple-element.7.db, f32[4,8,128]{2,1,0:T(8,128)} %get-tuple-element.8.sg, f32[4,2,8,8,128]{4,3,2,1,0:T(8,128)} %get-tuple-element.9.un, bf16[7168,256]{1,0:T(8,128)(2,1)} %bitcast.4, ...), custom_call_target="tpu_custom_call" | custom-call | tf_op jit(solution)/shard_map/backward/pallas_call | solution.py:553
  219.3 1.6 copy.15
  (1 shorter events, 0.0 us)
Async XLA Ops:
  0.6 0.9 copy-start

commit v6 on v5

--- a/solution.py
+++ b/solution.py
@@ -12,8 +12,8 @@
 META = 128
 LATE_TILES = (14, 18, 14)
 EARLY_TILES = (10,)
-LEAD, LAG = 1, 2
-EARLY_SLOTS = (1, 2, 3, 4, 5, 9, 12, 13, 14, 99)
+LEAD, LAG = 0, 2
+EARLY_SLOTS = (1, 2, 3, 4, 5, 9, 11, 12, 13, 14)
 MUL = 3
 BACKWARD_TILES = (8,) * 7
 BACKWARD_LAGS = (0, 2, 3, 3, 4, 5)

time: 223 us -> 225 us (level)
  no operation moved by 1% of the time
where the time goes in v6:
time: 225 us
  Pallas kernels  218 us (97%)
  local copies, waits for them, and re-layouts  2.55 us (1%)
  between operations  2.43 us (1%)
    pallas_call x1, Pallas kernels, forward(): pl.pallas_call(functools.partial(forward_kernel, chunks, early), out_shap...  131 us
    pallas_call x1, Pallas kernels, backward(): pl.pallas_call(functools.partial(backward_kernel, chunks), out_shape=(jax...  87.7 us

profile of v6, /device:TPU:1, one launch (start us, length us, event | category | flops | bytes accessed | tf_op | source)
XLA Modules:
  0.0 225.0 jit_solution(2169352297665255408)
XLA Ops:
  0.6 0.0 copy-start
  0.6 0.8 constant_dynamic-slice_fusion
  1.4 0.1 copy.12
  1.5 0.0 copy-done
  1.5 0.1 constant_dynamic-slice_fusion.1
  1.6 0.1 copy.11
  1.6 0.1 fusion.2
  1.7 1.7 maximum_maximum_fusion.blk
  3.4 130.6 %forward.1 = (bf16[512,256]{1,0:T(8,128)(2,1)}, bf16[512,256]{1,0:T(8,128)(2,1)}, f32[4,8,128]{2,1,0:T(8,128)}, f32[4,2,8,8,128]{4,3,2,1,0:T(8,128)}) custom-call(bf16[16,7296]{1,0:T(8,128)(2,1)} %maximum_maximum_fusion.blk, bf16[7168,256]{1,0:T(8,128)(2,1)} %bitcast.3, bf16[7168,256]{1,0:T(8,128)(2,1)} %bitcast.5, bf16[256,7168]{1,0:T(8,128)(2,1)} %bitcast.7), custom_call_target="tpu_custom_call" | custom-call | tf_op jit(solution)/shard_map/forward/pallas_call | solution.py:386
  134.0 87.7 %backward.1 = (bf16[8,7168]{1,0:T(8,128)(2,1)}, f32[1]{0:T(128)}) custom-call(bf16[512,256]{1,0:T(8,128)(2,1)} %get-tuple-element.6.da, bf16[512,256]{1,0:T(8,128)(2,1)} %get-tuple-element.7.db, f32[4,8,128]{2,1,0:T(8,128)} %get-tuple-element.8.sg, f32[4,2,8,8,128]{4,3,2,1,0:T(8,128)} %get-tuple-element.9.un, bf16[7168,256]{1,0:T(8,128)(2,1)} %bitcast.4, ...), custom_call_target="tpu_custom_call" | custom-call | tf_op jit(solution)/shard_map/backward/pallas_call | solution.py:553
  221.7 1.6 copy.15
  (1 shorter events, 0.0 us)
Async XLA Ops:
  0.6 0.9 copy-start

commit v7 on v6

--- a/solution.py
+++ b/solution.py
@@ -13,7 +13,7 @@
 LATE_TILES = (14, 18, 14)
 EARLY_TILES = (10,)
 LEAD, LAG = 0, 2
-EARLY_SLOTS = (1, 2, 3, 4, 5, 9, 11, 12, 13, 14)
+EARLY_SLOTS = (1, 2, 3, 4, 5, 9, 12, 13, 14, 99)
 MUL = 3
 BACKWARD_TILES = (8,) * 7
 BACKWARD_LAGS = (0, 2, 3, 3, 4, 5)

time: 225 us -> 224 us (level)
  no operation moved by 1% of the time
where the time goes in v7:
time: 224 us; the launch traced here: 223 us
  Pallas kernels  217 us (97%)
  local copies, waits for them, and re-layouts  2.55 us (1%)
  between operations  2.43 us (1%)
    pallas_call x1, Pallas kernels, forward(): pl.pallas_call(functools.partial(forward_kernel, chunks, early), out_shap...  131 us
    pallas_call x1, Pallas kernels, backward(): pl.pallas_call(functools.partial(backward_kernel, chunks), out_shape=(jax...  86.1 us

profile of v7, /device:TPU:1, one launch (start us, length us, event | category | flops | bytes accessed | tf_op | source)
XLA Modules:
  0.0 223.3 jit_solution(10112465852603926817)
XLA Ops:
  0.6 0.0 copy-start
  0.6 0.8 constant_dynamic-slice_fusion
  1.4 0.1 copy.12
  1.5 0.0 copy-done
  1.5 0.1 constant_dynamic-slice_fusion.1
  1.6 0.1 copy.11
  1.6 0.1 fusion.2
  1.7 1.7 maximum_maximum_fusion.blk
  3.4 130.5 %forward.1 = (bf16[512,256]{1,0:T(8,128)(2,1)}, bf16[512,256]{1,0:T(8,128)(2,1)}, f32[4,8,128]{2,1,0:T(8,128)}, f32[4,2,8,8,128]{4,3,2,1,0:T(8,128)}) custom-call(bf16[16,7296]{1,0:T(8,128)(2,1)} %maximum_maximum_fusion.blk, bf16[7168,256]{1,0:T(8,128)(2,1)} %bitcast.3, bf16[7168,256]{1,0:T(8,128)(2,1)} %bitcast.5, bf16[256,7168]{1,0:T(8,128)(2,1)} %bitcast.7), custom_call_target="tpu_custom_call" | custom-call | tf_op jit(solution)/shard_map/forward/pallas_call | solution.py:386
  133.9 86.1 %backward.1 = (bf16[8,7168]{1,0:T(8,128)(2,1)}, f32[1]{0:T(128)}) custom-call(bf16[512,256]{1,0:T(8,128)(2,1)} %get-tuple-element.6.da, bf16[512,256]{1,0:T(8,128)(2,1)} %get-tuple-element.7.db, f32[4,8,128]{2,1,0:T(8,128)} %get-tuple-element.8.sg, f32[4,2,8,8,128]{4,3,2,1,0:T(8,128)} %get-tuple-element.9.un, bf16[7168,256]{1,0:T(8,128)(2,1)} %bitcast.4, ...), custom_call_target="tpu_custom_call" | custom-call | tf_op jit(solution)/shard_map/backward/pallas_call | solution.py:553
  220.0 1.6 copy.15
  (1 shorter events, 0.0 us)
Async XLA Ops:
  0.6 0.9 copy-start
